TPU v7x, 32 devices: a whole 2x2x4 slice. The times are simulated.
32 devices in a mesh: group: 2 (over y), replica: 4 (over z), tensor: 2 (over x), sub: 2 (over core).
Axes of the slice: x: 2, y: 2, z: 4, core: 2. Of those that a mesh axis runs over, the one named last changes fastest.
Arguments:
- queries: bfloat16 [2048, 4096], P(('group', 'replica'), ('tensor', 'sub')), parts along dimension 0, may hold values from -20 to 20
- incoming_keys: bfloat16 [2048, 512], P(('group', 'replica'), 'tensor'), parts along dimension 0, may hold values from -4 to 4
- incoming_values: bfloat16 [2048, 512], P(('group', 'replica'), 'tensor'), parts along dimension 0, may hold values from -6 to 6
- cached_key_rows: bfloat16 [2048, 32, 512], P(('group', 'replica'), None, 'tensor'), parts along dimension 0, may hold values from -4 to 4
- cached_value_rows: bfloat16 [2048, 32, 512], P(('group', 'replica'), None, 'tensor'), parts along dimension 0, may hold values from -6 to 6
- cache_length: int32 [2048], P(('group', 'replica')), parts along dimension 0, may hold values from 1 to 32, as said below
- adapter_of_row: int32 [2048], P(('group', 'replica')), parts along dimension 0, may hold values from 0 to 15, as said below
- adapter_slot_table: int32 [32], P('group'), parts along dimension 0, may hold values from 0 to 15, as said below
- output_projection: bfloat16 [4096, 8192], P(('tensor', 'sub')), may hold values from -0.1875 to 0.1875
- adapter_down_weights: bfloat16 [16, 4096, 64], P('replica', ('tensor', 'sub')), may hold values from -0.1875 to 0.1875
- adapter_up_weights: bfloat16 [16, 64, 8192], P('replica', None, ('tensor', 'sub')), may hold values from -1.5 to 1.5
Outputs:
- projected: bfloat16 [2048, 8192], P(('group', 'replica'), ('tensor', 'sub')), parts along dimension 0
There are 2 independent parts, one for each index of `group`. A program takes and returns all parts, laid end to end along the dimension named above; an argument that names none is the same for every part. Nothing has to cross between parts.
Inputs may be any that keep to these rules, and one draw needn't show every extreme that they name: A permutation: adapter a is stored in slot adapter_slot_table[a]. `adapter_of_row`: of the 256 rows of one replica, at most 64 use adapters stored on any one replica; in every draw some replica stores the adapters of exactly 64 rows of every replica. `cache_length`: some row has exactly 32.
All inputs are finite; a program needn't handle non-finite values.
Results may differ from a plain program's by a relative error of at most 0.0085.
Values may be sent and summed in bfloat16 or wider, within the bound.
A program may use at most 128 MiB of HBM per device.

v0:
```python
import jax
import jax.numpy as jnp
from jax import lax
from jax.sharding import PartitionSpec as P

QUERY_HEADS = 32
KV_HEADS = 4
HEAD_WIDTH = 128
CAP = 64


def attend_local(
    queries, incoming_keys, incoming_values, cached_key_rows, cached_value_rows, cache_length
):
    row_count = queries.shape[0]
    feat_count = queries.shape[1]
    local_heads = feat_count // HEAD_WIDTH
    group_size = QUERY_HEADS // KV_HEADS
    kv_span = max(1, local_heads // group_size)
    per_kv = min(group_size, local_heads)
    first_kv = lax.axis_index("sub") * local_heads // group_size
    context = cached_key_rows.shape[1]
    kv_local = cached_key_rows.shape[2] // HEAD_WIDTH

    def pick_heads(stored):
        shaped = stored.reshape(stored.shape[:-1] + (kv_local, HEAD_WIDTH))
        return lax.dynamic_slice_in_dim(shaped, first_kv, kv_span, shaped.ndim - 2)

    keys_old = pick_heads(cached_key_rows)
    values_old = pick_heads(cached_value_rows)
    keys_now = pick_heads(incoming_keys)
    values_now = pick_heads(incoming_values)
    query_all = queries.reshape(row_count, kv_span, per_kv, HEAD_WIDTH)
    score_scale = HEAD_WIDTH ** (-0.5)
    scores = (
        jnp.einsum("rkgd,rckd->rkgc", query_all, keys_old, preferred_element_type=jnp.float32)
        * score_scale
    )
    allowed = lax.broadcasted_iota(jnp.int32, (row_count, context), 1) < cache_length[:, None]
    scores = jnp.where(allowed[:, None, None, :], scores, -1e30)
    fresh = (
        jnp.einsum("rkgd,rkd->rkg", query_all, keys_now, preferred_element_type=jnp.float32)
        * score_scale
    )
    highest = jnp.maximum(jnp.max(scores, axis=3), fresh)
    weights = jnp.exp(scores - highest[..., None])
    fresh_weight = jnp.exp(fresh - highest)
    weight_total = jnp.sum(weights, axis=3) + fresh_weight
    mixed = jnp.einsum(
        "rkgc,rckd->rkgd",
        weights.astype(jnp.bfloat16),
        values_old,
        preferred_element_type=jnp.float32,
    )
    mixed = mixed + jnp.einsum(
        "rkg,rkd->rkgd",
        fresh_weight.astype(jnp.bfloat16),
        values_now,
        preferred_element_type=jnp.float32,
    )
    attended = (mixed / weight_total[..., None]).astype(jnp.bfloat16)
    return attended.reshape(row_count, feat_count)


def grouped_product(rows_by_adapter, weights, group_sizes, leading_extent):
    total_rows = rows_by_adapter.shape[0]
    shifted = jnp.roll(rows_by_adapter, -leading_extent, axis=0)
    result = lax.ragged_dot(shifted, weights, group_sizes, preferred_element_type=jnp.float32)
    used = lax.broadcasted_iota(jnp.int32, (total_rows, 1), 0) < jnp.sum(group_sizes)
    result = jnp.where(used, result, 0.0)
    return jnp.roll(result, leading_extent, axis=0)


def on_device(
    queries,
    incoming_keys,
    incoming_values,
    cached_key_rows,
    cached_value_rows,
    cache_length,
    adapter_of_row,
    adapter_slot_table,
    output_projection,
    adapter_down_weights,
    adapter_up_weights,
):
    row_count = queries.shape[0]
    feat_count = queries.shape[1]
    attended = attend_local(
        queries, incoming_keys, incoming_values, cached_key_rows, cached_value_rows, cache_length
    )
    partial_out = jnp.dot(attended, output_projection, preferred_element_type=jnp.float32)
    base = lax.psum_scatter(partial_out, ("tensor", "sub"), scatter_dimension=1, tiled=True)
    output_columns = adapter_up_weights.shape[2]
    adp_local = adapter_down_weights.shape[0]
    adapter_count = adapter_slot_table.shape[0]
    matched = adapter_of_row[:, None] == lax.broadcasted_iota(
        jnp.int32, (row_count, adapter_count), 1
    )
    slot_of_row = jnp.sum(jnp.where(matched, adapter_slot_table[None, :], 0), axis=1)
    owners = lax.axis_size("replica")
    owner_of_row = slot_of_row // adp_local
    local_id = slot_of_row - owner_of_row * adp_local
    by_owner = (
        owner_of_row[:, None] == lax.broadcasted_iota(jnp.int32, (row_count, owners), 1)
    ).astype(jnp.int32)
    earlier = jnp.cumsum(by_owner, axis=0) - by_owner
    position = jnp.sum(earlier * by_owner, axis=1)
    target = owner_of_row * CAP + position
    slot_total = owners * CAP
    route_map = (
        target[:, None] == lax.broadcasted_iota(jnp.int32, (row_count, slot_total), 1)
    ).astype(jnp.bfloat16)
    outgoing = jnp.einsum("rs,rf->sf", route_map, attended, preferred_element_type=jnp.float32)
    outgoing = outgoing.astype(jnp.bfloat16).reshape(owners, CAP, feat_count)
    labels = jnp.einsum(
        "rs,r->s",
        route_map,
        (local_id + 1).astype(jnp.bfloat16),
        preferred_element_type=jnp.float32,
    )
    labels = labels.astype(jnp.bfloat16).reshape(owners, CAP)
    arrived, arrived_labels = (
        lax.all_to_all(outgoing, "replica", split_axis=0, concat_axis=0, tiled=True),
        lax.all_to_all(labels, "replica", split_axis=0, concat_axis=0, tiled=True),
    )
    arrived_rows = arrived.reshape(slot_total, feat_count)
    label_ids = arrived_labels.reshape(slot_total).astype(jnp.int32)
    sort_keys = jnp.where(label_ids == 0, adp_local + 1, label_ids)
    order_in = jnp.argsort(sort_keys, stable=True)
    inverse_in = jnp.argsort(order_in, stable=True)
    sorted_in = arrived_rows[order_in]
    wanted = lax.broadcasted_iota(jnp.int32, (1, adp_local), 1) + 1
    sizes_in = jnp.sum((label_ids[:, None] == wanted).astype(jnp.int32), axis=0)
    rank_part = grouped_product(sorted_in, adapter_down_weights, sizes_in, 0)
    shrunk_in = lax.psum(rank_part, ("tensor", "sub")).astype(jnp.bfloat16)
    delta_sorted = grouped_product(shrunk_in, adapter_up_weights, sizes_in, 0).astype(jnp.bfloat16)
    delta_in = delta_sorted[inverse_in].reshape(owners, CAP, output_columns)
    returned = lax.all_to_all(delta_in, "replica", split_axis=0, concat_axis=0, tiled=True)
    delta = jnp.einsum(
        "rs,sc->rc",
        route_map,
        returned.reshape(slot_total, output_columns),
        preferred_element_type=jnp.float32,
    )
    delta = delta.astype(jnp.bfloat16)
    return (base + delta.astype(jnp.float32)).astype(jnp.bfloat16)


def solution(mesh):
    return jax.shard_map(
        on_device,
        mesh=mesh,
        in_specs=(
            P(("group", "replica"), ("tensor", "sub")),
            P(("group", "replica"), "tensor"),
            P(("group", "replica"), "tensor"),
            P(("group", "replica"), None, "tensor"),
            P(("group", "replica"), None, "tensor"),
            P(("group", "replica")),
            P(("group", "replica")),
            P("group"),
            P(("tensor", "sub"), None),
            P("replica", ("tensor", "sub"), None),
            P("replica", None, ("tensor", "sub")),
        ),
        out_specs=P(("group", "replica"), ("tensor", "sub")),
        check_vma=False,
    )
```

profile of v0, /device:TPU:0, one launch (start us, length us, event | category | flops | bytes accessed | tf_op | source)
XLA Modules:
  0.0 156.4 jit_solution(1407513192629965480)
XLA Ops:
  6.5 0.0 reduce-scatter.2.cloned.1.call-start
  6.5 6.9 %reshape.166 = bf16[256,32,2,128]{3,2,1,0:T(2,128)(2,1)} reshape(bf16[256,32,256]{2,1,0:T(8,128)(2,1)} %param.14) | data formatting | bytes 8388608 | tf_op jit(solution)/shard_map/reshape | solution.py:26
  13.5 0.0 copy-start.1
  13.5 0.0 copy-start.4
  13.5 0.0 copy-start.2
  13.5 7.0 %reshape.171 = bf16[256,32,2,128]{3,2,1,0:T(2,128)(2,1)} reshape(bf16[256,32,256]{2,1,0:T(8,128)(2,1)} %param.15) | data formatting | bytes 8388608 | tf_op jit(solution)/shard_map/reshape | solution.py:26
  20.5 0.0 copy-done.1
  20.5 0.1 copy.55
  20.6 0.0 copy-done.4
  20.6 0.1 iota_compare_fusion.4
  20.7 0.0 copy-done.2
  20.7 0.1 copy.42
  20.8 0.1 copy.43
  20.9 13.0 %constant_dynamic-slice_fusion.1 = (bf16[256,32,1,128]{3,2,1,0:T(2,128)(2,1)}, bf16[256,32,1,128]{3,2,1,0:T(2,128)(2,1)S(1)}) fusion(bf16[256,32,2,128]{3,2,1,0:T(2,128)(2,1)} %reshape.171, s32[]{:T(128)S(6)} %select_n.57, bf16[256,32,2,128]{3,2,1,0:T(2,128)(2,1)} %reshape.166), kind=kLoop, calls=%fused_computation.72 | loop fusion | bytes 8388612 | tf_op jit(solution)/shard_map/dynamic_slice | solution.py:27
  33.9 0.0 copy-start.3
  33.9 0.4 fusion.24
  34.3 1.3 fusion.31
  35.6 0.7 fusion.11
  36.4 0.0 copy-done.3
  36.4 0.1 constant_dynamic-slice_fusion
  36.6 3.1 %fusion.10 = bf16[256,8,128]{2,1,0:T(8,128)(2,1)S(1)} fusion(bf16[256,32,1,128]{3,2,1,0:T(2,128)(2,1)} %get-tuple-element.25, f32[256,8,32]{2,1,0:T(8,128)S(1)} %get-tuple-element.24, f32[256,8]{1,0:T(8,128)S(1)} %get-tuple-element.22, f32[256,128]{1,0:T(8,128)S(1)} %fusion.26, f32[256,8]{1,0:T(8,128)S(1)} %get-tuple-element.21, ...), kind=kOutput, calls=%fused_computation.17 | convolution fusion | flops 17956864 | bytes 3039232 | tf_op jit(solution)/shard_map/rkgc,rckd->rkgd/dot_general | solution.py:49
  39.7 12.5 %fusion.15 = f32[256,8192]{1,0:T(8,128)} fusion(bf16[1024,8192]{1,0:T(8,128)(2,1)} %param.19, bf16[32,8,8,128]{3,2,1,0:T(8,128)(2,1)S(1)} %bitcast.80), kind=kOutput, calls=%fused_computation.22 | convolution fusion | flops 4294967296 | bytes 25690112 | tf_op jit(solution)/shard_map/dot_general | solution.py:92
  52.2 0.0 copy-start.5
  52.2 0.0 copy-start.6
  52.2 0.0 copy-start
  52.2 0.0 reduce-scatter.2.cloned.1.call-update
  52.2 0.6 copy-done.5
  52.8 0.0 copy-done.6
  52.8 0.1 select_reduce_fusion
  53.0 1.2 reduce-window.6
  54.2 0.1 slice.12
  54.3 0.1 copy.46
  54.4 0.1 copy.47
  54.5 0.1 add_bitcast_fusion
  54.6 0.2 fusion.20
  54.9 0.7 all_to_all.16
  55.5 6.3 %all-to-all-start = ((bf16[4,1,64]{2,1,0:T(2,128)(2,1)}), bf16[4,1,64]{2,1,0:T(2,128)(2,1)S(1)}, u32[]{:S(2)}, u32[]{:S(2)}) async-start(bf16[4,1,64]{2,1,0:T(2,128)(2,1)} %all_to_all.16), calls=%async_computation.1 | async-start | bytes 4096 | tf_op jit(solution)/shard_map/all_to_all | solution.py:125
  61.9 1.2 convolution_convert_fusion.1
  63.1 0.0 copy-done
  63.1 1.3 copy.49
  64.4 3.0 %all-to-all-done = bf16[4,1,64]{2,1,0:T(2,128)(2,1)S(1)} async-done(((bf16[4,1,64]{2,1,0:T(2,128)(2,1)}), bf16[4,1,64]{2,1,0:T(2,128)(2,1)S(1)}, u32[]{:S(2)}, u32[]{:S(2)}) %all-to-all-start) | async-done | bytes 544 | tf_op jit(solution)/shard_map/all_to_all | solution.py:125
  67.4 3.5 %all-to-all-start.1 = ((bf16[4,64,1024]{2,1,0:T(8,128)(2,1)}), bf16[4,64,1024]{2,1,0:T(8,128)(2,1)S(1)}, u32[]{:S(2)}, u32[]{:S(2)}) async-start(bf16[4,64,1024]{2,1,0:T(8,128)(2,1)} %bitcast.13), calls=%async_computation.2 | async-start | bytes 1048576 | tf_op jit(solution)/shard_map/all_to_all | solution.py:124
  70.9 0.1 reshape.182
  71.0 0.7 convert_reduce_fusion.1
  71.7 1.3 ragged-dot-metadata
  73.1 3.1 %sort.31 = (s32[256]{0:T(256)}, s32[256]{0:T(256)S(1)}) sort(s32[256]{0:T(256)S(1)} %compare_select_fusion.2, s32[256]{0:T(256)S(1)} %iota.54), dimensions={0}, to_apply=%region_8.9 | sort | flops 2048 | bytes 4096 | tf_op jit(solution)/shard_map/jit(argsort)/sort | solution.py:130
  76.2 3.1 %sort.32 = (s32[256]{0:T(256)}, s32[256]{0:T(256)S(1)}) sort(s32[256]{0:T(256)S(1)} %get-tuple-element.7, s32[256]{0:T(256)S(1)} %iota.55), dimensions={0}, to_apply=%region_11.12 | sort | flops 2048 | bytes 4096 | tf_op jit(solution)/shard_map/jit(argsort)/sort | solution.py:131
  79.4 0.6 iota_compare_fusion.7
  80.1 4.0 %all-to-all-done.1 = bf16[4,64,1024]{2,1,0:T(8,128)(2,1)S(1)} async-done(((bf16[4,64,1024]{2,1,0:T(8,128)(2,1)}), bf16[4,64,1024]{2,1,0:T(8,128)(2,1)S(1)}, u32[]{:S(2)}, u32[]{:S(2)}) %all-to-all-start.1) | async-done | bytes 524320 | tf_op jit(solution)/shard_map/all_to_all | solution.py:124
  84.1 2.0 %gather_fusion = bf16[256,1024]{1,0:T(8,128)(2,1)} fusion(bf16[256,1024]{1,0:T(8,128)(2,1)S(1)} %bitcast.77, s32[1024]{0:T(1024)S(1)} %pad_clamp_fusion.1), kind=kCustom, calls=%fused_computation | custom fusion | bytes 1049600 | tf_op jit(solution)/shard_map/gather | solution.py:132
  86.0 5.8 %ragged-dot-none.1 = f32[256,64]{1,0:T(8,128)} custom-call(s32[1]{0:T(128)} %get-tuple-element.9, s32[5]{0:T(128)} %get-tuple-element.10, s32[4]{0:T(128)} %get-tuple-element.11, s32[4]{0:T(128)} %get-tuple-element.12, s32[1]{0:T(128)} %get-tuple-element.9, bf16[256,1024]{1,0:T(8,128)(2,1)} %gather_fusion, bf16[4,1024,64]{2,1,0:T(8,128)(2,1)} %copy.49), custom_call_target="tpu_custom_call" | custom-call | flops 33554432 | bytes 1114128 | tf_op jit(solution)/shard_map/ragged_dot_general/ragged-dot-none
  91.8 1.0 broadcast_select_fusion
  92.8 15.3 %psum.7 = bf16[256,64]{1,0:T(8,128)(2,1)} all-reduce(f32[256,64]{1,0:T(8,128)S(1)} %broadcast_select_fusion), channel_id=1, replica_groups=mesh['group'=2,'replica'=4,'tensor'=2,'sub'=2] {'tensor','sub'}, use_global_device_ids=true, to_apply=%region_10.11 | all-reduce | flops 16384 | bytes 98304 | tf_op jit(solution)/shard_map/psum | solution.py:136
  108.1 6.6 %ragged-dot-none = f32[256,2048]{1,0:T(8,128)} custom-call(s32[1]{0:T(128)} %get-tuple-element.9, s32[5]{0:T(128)} %get-tuple-element.10, s32[4]{0:T(128)} %get-tuple-element.11, s32[4]{0:T(128)} %get-tuple-element.12, s32[1]{0:T(128)} %get-tuple-element.9, bf16[256,64]{1,0:T(8,128)(2,1)} %psum.7, bf16[4,64,2048]{2,1,0:T(8,128)(2,1)} %param.21), custom_call_target="tpu_custom_call" | custom-call | flops 67108864 | bytes 3178512 | tf_op jit(solution)/shard_map/ragged_dot_general/ragged-dot-none
  114.7 1.8 %select_convert_fusion = bf16[256,2048]{1,0:T(8,128)(2,1)S(1)} fusion(f32[256,2048]{1,0:T(8,128)} %ragged-dot-none, pred[256]{0:T(512)(128)(4,1)S(1)} %iota_compare_fusion.7), kind=kLoop, calls=%fused_computation.10 | loop fusion | flops 524288 | bytes 3145984 | tf_op jit(solution)/shard_map/convert_element_type | solution.py:137
  116.5 1.4 gather_fusion.1
  117.9 28.6 %all_to_all.20 = bf16[4,64,2048]{2,1,0:T(8,128)(2,1)S(1)} all-to-all(bf16[4,64,2048]{2,1,0:T(8,128)(2,1)S(1)} %bitcast.79), channel_id=1, replica_groups=mesh['group'=2,'replica'=4,'tensor'=2,'sub'=2] {'replica'}, dimensions={0} | all-to-all | bytes 2097152 | tf_op jit(solution)/shard_map/all_to_all | solution.py:139
  146.5 0.0 reduce-scatter.2.cloned.1.call-done
  146.5 3.1 %fusion.2 = bf16[256,2048]{1,0:T(8,128)(2,1)} fusion(f32[256,2048]{1,0:T(8,128)} %reduce-scatter.2.cloned.1.call-done, bf16[256,2048]{1,0:T(8,128)(2,1)S(1)} %bitcast.78, s32[256]{0:T(256)S(1)} %multiply_add_fusion), kind=kOutput, calls=%fused_computation.5 | convolution fusion | flops 270598144 | bytes 4195328 | tf_op jit(solution)/shard_map/rs,sc->rc/dot_general | solution.py:140
  (23 shorter events, 0.3 us)
Async XLA Ops:
  6.5 139.9 %reduce-scatter.2.cloned.1.call-start = ((), (), s32[]{:S(2)}) async-start(), calls=%async_computation.4 | async-start | bytes 10485760 | tf_op jit(solution)/shard_map/reduce_scatter | solution.py:93
  13.5 7.0 %copy-start.1 = (bf16[256,1024]{1,0:T(8,128)(2,1)S(1)}, bf16[256,1024]{1,0:T(8,128)(2,1)}, u32[]{:S(2)}) copy-start(bf16[256,1024]{1,0:T(8,128)(2,1)} %param.11) | copy-start | bytes 1572868
  13.5 7.1 %copy-start.4 = (s32[256]{0:T(256)S(1)}, s32[256]{0:T(256)}, u32[]{:S(2)}) copy-start(s32[256]{0:T(256)} %param.16) | copy-start | bytes 3076
  13.5 7.2 %copy-start.2 = (bf16[256,256]{1,0:T(8,128)(2,1)S(1)}, bf16[256,256]{1,0:T(8,128)(2,1)}, u32[]{:S(2)}) copy-start(bf16[256,256]{1,0:T(8,128)(2,1)} %param.12) | copy-start | bytes 393220
  33.9 2.5 %copy-start.3 = (bf16[256,256]{1,0:T(8,128)(2,1)S(1)}, bf16[256,256]{1,0:T(8,128)(2,1)}, u32[]{:S(2)}) copy-start(bf16[256,256]{1,0:T(8,128)(2,1)} %param.13) | copy-start | bytes 393220
  52.2 0.7 copy-start.5
  52.2 0.7 copy-start.6
  52.2 10.9 %copy-start = (bf16[4,1024,64]{1,2,0:T(8,128)(2,1)S(1)}, bf16[4,1024,64]{1,2,0:T(8,128)(2,1)}, u32[]{:S(2)}) copy-start(bf16[4,1024,64]{1,2,0:T(8,128)(2,1)} %param.20) | copy-start | bytes 1572868
  55.5 11.9 %all-to-all-start = ((bf16[4,1,64]{2,1,0:T(2,128)(2,1)}), bf16[4,1,64]{2,1,0:T(2,128)(2,1)S(1)}, u32[]{:S(2)}, u32[]{:S(2)}) async-start(bf16[4,1,64]{2,1,0:T(2,128)(2,1)} %all_to_all.16), calls=%async_computation.1 | async-start | bytes 4096 | tf_op jit(solution)/shard_map/all_to_all | solution.py:125
  67.4 16.6 %all-to-all-start.1 = ((bf16[4,64,1024]{2,1,0:T(8,128)(2,1)}), bf16[4,64,1024]{2,1,0:T(8,128)(2,1)S(1)}, u32[]{:S(2)}, u32[]{:S(2)}) async-start(bf16[4,64,1024]{2,1,0:T(8,128)(2,1)} %bitcast.13), calls=%async_computation.2 | async-start | bytes 1048576 | tf_op jit(solution)/shard_map/all_to_all | solution.py:124
Sparse Core Ops, SparseCore 0:
  52.3 76.5 reduce-scatter.1
where the time goes:
time: 157 us; the launch traced here: 156 us
  blocking collectives  43.9 us (28%)
  local copies, waits for them, and re-layouts  33.8 us (22%)
  matrix products  21.8 us (14%)
  Pallas kernels  13.7 us (9%)
  between operations  13.6 us (9%)
  other arithmetic  12.8 us (8%)
  starting transfers between devices  9.81 us (6%)
  waiting for transfers between devices  7 us (4%)
    all_to_all x1, blocking collectives, on_device(): lax.all_to_all(delta_in, 'replica', split_axis=0, concat_axis=0, tiled=True)  28.6 us
    psum x1, blocking collectives, on_device(): shrunk_in = lax.psum(rank_part, ('tensor', 'sub')).astype(jnp.bfloat16)  15.3 us
    reshape x3, local copies, waits for them, and re-layouts, pick_heads(): shaped = stored.reshape(stored.shape[:-1] + (kv_local, HEAD_WIDTH))  13.9 us
    dynamic_slice x4, local copies, waits for them, and re-layouts, pick_heads(): return lax.dynamic_slice_in_dim(shaped, first_kv, kv_span, shaped.ndim - 2)  13.2 us
    dot_general x1, matrix products, on_device(): jnp.dot(attended, output_projection, preferred_element_type=jnp.float32)  12.5 us
    another operation x2, Pallas kernels  12.4 us
    all_to_all x1, starting transfers between devices, on_device(): lax.all_to_all(labels, 'replica', split_axis=0, concat_axis=0, tiled=True)  6.32 us
    all_to_all x1, waiting for transfers between devices, on_device(): lax.all_to_all(outgoing, 'replica', split_axis=0, concat_axis=0, tiled=True)  4 us
  transfers between devices with their start and end apart: 3, of which 2 were waited for; matrix products, arithmetic and copies ran while one was open for 12% of the time, Pallas kernels for 9%

commit v1 on v0

--- a/solution.py
+++ b/solution.py
@@ -1,65 +1,113 @@
 import jax
 import jax.numpy as jnp
 from jax import lax
+from jax.experimental import pallas as pl
+from jax.experimental.pallas import tpu as pltpu
 from jax.sharding import PartitionSpec as P
 
 QUERY_HEADS = 32
 KV_HEADS = 4
 HEAD_WIDTH = 128
 CAP = 64
+LANES = 128
+
+
+def attend_kernel(
+    column_ref, length_ref, query_ref, key_now_ref, value_now_ref, key_ref, value_ref, out_ref
+):
+    block = query_ref.shape[0]
+    heads = query_ref.shape[1] // HEAD_WIDTH
+    context = key_ref.shape[1]
+    rows = LANES // heads
+    copies = LANES // context
+    first_row = pl.program_id(0) * block
+    lane = lax.broadcasted_iota(jnp.int32, (1, LANES), 1)
+    lane_row = lax.rem(lane, rows)
+    row_masks = [lane_row == r for r in range(rows)]
+    place = lax.broadcasted_iota(jnp.int32, (context, LANES), 0)
+    side = lax.broadcasted_iota(jnp.int32, (LANES, LANES), 0)
+    across = lax.broadcasted_iota(jnp.int32, (LANES, LANES), 1)
+    fresh_mask = side == lax.rem(across, rows)
+    offset = lax.rem(side, rows) - across // context
+    score_scale = HEAD_WIDTH ** (-0.5)
+    contract_last = (((1,), (1,)), ((), ()))
+    for group in range(block // rows):
+        at = slice(group * rows, (group + 1) * rows)
+        stacked = jnp.concatenate(
+            [query_ref[at, h * HEAD_WIDTH : (h + 1) * HEAD_WIDTH] for h in range(heads)], axis=0
+        )
+        keys = key_ref[at].reshape(rows * context, HEAD_WIDTH)
+        wide = lax.dot_general(
+            keys, stacked, contract_last, preferred_element_type=jnp.float32
+        ).reshape(rows, context, LANES)
+        lengths = jnp.zeros((1, LANES), jnp.int32)
+        scores = wide[0]
+        for r in range(rows):
+            lengths = jnp.where(row_masks[r], length_ref[first_row + group * rows + r], lengths)
+            scores = jnp.where(row_masks[r], wide[r], scores)
+        now = lax.dot_general(
+            key_now_ref[at], stacked, contract_last, preferred_element_type=jnp.float32
+        )
+        fresh = jnp.sum(jnp.where(fresh_mask[:rows], now, 0.0), axis=0, keepdims=True)
+        fresh = fresh * score_scale
+        scores = jnp.where(place < lengths, scores * score_scale, -1e30)
+        highest = jnp.maximum(jnp.max(scores, axis=0, keepdims=True), fresh)
+        weights = jnp.exp(scores - highest)
+        fresh_weight = jnp.exp(fresh - highest)
+        total = jnp.sum(weights, axis=0, keepdims=True) + fresh_weight
+        turned = jnp.transpose(jnp.concatenate([weights] * copies, axis=0))
+        extra = jnp.where(side < rows, jnp.where(fresh_mask, fresh_weight, 0.0), total)
+        extra = jnp.transpose(extra)
+        spread = jnp.concatenate(
+            [
+                jnp.where(offset == t * copies, turned, 0.0).astype(jnp.bfloat16)
+                for t in range(rows // copies)
+            ],
+            axis=1,
+        )
+        values = value_ref[at].reshape(rows * context, HEAD_WIDTH)
+        mixed = jnp.dot(spread, values, preferred_element_type=jnp.float32)
+        mixed = mixed + jnp.dot(
+            extra[:, :rows].astype(jnp.bfloat16),
+            value_now_ref[at],
+            preferred_element_type=jnp.float32,
+        )
+        attended = (mixed / extra[:, rows : rows + 1]).astype(jnp.bfloat16)
+        for h in range(heads):
+            out_ref[at, h * HEAD_WIDTH : (h + 1) * HEAD_WIDTH] = attended[h * rows : (h + 1) * rows]
 
 
 def attend_local(
     queries, incoming_keys, incoming_values, cached_key_rows, cached_value_rows, cache_length
 ):
-    row_count = queries.shape[0]
-    feat_count = queries.shape[1]
-    local_heads = feat_count // HEAD_WIDTH
-    group_size = QUERY_HEADS // KV_HEADS
-    kv_span = max(1, local_heads // group_size)
-    per_kv = min(group_size, local_heads)
-    first_kv = lax.axis_index("sub") * local_heads // group_size
+    row_count, feat_count = queries.shape
     context = cached_key_rows.shape[1]
-    kv_local = cached_key_rows.shape[2] // HEAD_WIDTH
-
-    def pick_heads(stored):
-        shaped = stored.reshape(stored.shape[:-1] + (kv_local, HEAD_WIDTH))
-        return lax.dynamic_slice_in_dim(shaped, first_kv, kv_span, shaped.ndim - 2)
-
-    keys_old = pick_heads(cached_key_rows)
-    values_old = pick_heads(cached_value_rows)
-    keys_now = pick_heads(incoming_keys)
-    values_now = pick_heads(incoming_values)
-    query_all = queries.reshape(row_count, kv_span, per_kv, HEAD_WIDTH)
-    score_scale = HEAD_WIDTH ** (-0.5)
-    scores = (
-        jnp.einsum("rkgd,rckd->rkgc", query_all, keys_old, preferred_element_type=jnp.float32)
-        * score_scale
-    )
-    allowed = lax.broadcasted_iota(jnp.int32, (row_count, context), 1) < cache_length[:, None]
-    scores = jnp.where(allowed[:, None, None, :], scores, -1e30)
-    fresh = (
-        jnp.einsum("rkgd,rkd->rkg", query_all, keys_now, preferred_element_type=jnp.float32)
-        * score_scale
-    )
-    highest = jnp.maximum(jnp.max(scores, axis=3), fresh)
-    weights = jnp.exp(scores - highest[..., None])
-    fresh_weight = jnp.exp(fresh - highest)
-    weight_total = jnp.sum(weights, axis=3) + fresh_weight
-    mixed = jnp.einsum(
-        "rkgc,rckd->rkgd",
-        weights.astype(jnp.bfloat16),
-        values_old,
-        preferred_element_type=jnp.float32,
-    )
-    mixed = mixed + jnp.einsum(
-        "rkg,rkd->rkgd",
-        fresh_weight.astype(jnp.bfloat16),
-        values_now,
-        preferred_element_type=jnp.float32,
-    )
-    attended = (mixed / weight_total[..., None]).astype(jnp.bfloat16)
-    return attended.reshape(row_count, feat_count)
+    heads = feat_count // HEAD_WIDTH
+    first_kv = lax.axis_index("sub") * heads // (QUERY_HEADS // KV_HEADS)
+    column = first_kv.astype(jnp.int32).reshape(1)
+    block = 64
+    now_spec = pl.BlockSpec((block, HEAD_WIDTH), lambda i, c, n: (i, c[0]))
+    old_spec = pl.BlockSpec((block, context, HEAD_WIDTH), lambda i, c, n: (i, 0, c[0]))
+    row_spec = pl.BlockSpec((block, feat_count), lambda i, c, n: (i, 0))
+    return pl.pallas_call(
+        attend_kernel,
+        grid_spec=pltpu.PrefetchScalarGridSpec(
+            num_scalar_prefetch=2,
+            grid=(row_count // block,),
+            in_specs=[row_spec, now_spec, now_spec, old_spec, old_spec],
+            out_specs=row_spec,
+        ),
+        out_shape=jax.ShapeDtypeStruct((row_count, feat_count), jnp.bfloat16),
+        name="attend",
+    )(
+        column,
+        cache_length,
+        queries,
+        incoming_keys,
+        incoming_values,
+        cached_key_rows,
+        cached_value_rows,
+    )
 
 
 def grouped_product(rows_by_adapter, weights, group_sizes, leading_extent):

time: 157 us -> 134 us (0.85)
  local copies, waits for them, and re-layouts: 33.8 us -> 6.37 us
  Pallas kernels: 13.7 us -> 22.7 us
  matrix products: 21.8 us -> 18.2 us
    reshape x3 -> x0, local copies, waits for them, and re-layouts: 13.9 us -> none  [pick_heads(): shaped = stored.reshape(stored.shape[:-1] + (kv_local, HEAD_WIDTH))]
    dynamic_slice x4 -> x0, local copies, waits for them, and re-layouts: 13.2 us -> none  [pick_heads(): return lax.dynamic_slice_in_dim(shaped, first_kv, kv_span, shaped.ndim - 2)]
    pallas_call x0 -> x1, Pallas kernels: none -> 9 us  [attend_local(): pl.pallas_call(attend_kernel, grid_spec=pltpu.PrefetchScalarGridSpec(num_...]
    dot_general x3 -> x0, matrix products: 4.77 us -> none  [the longest x1 3.09 us: attend_local(): jnp.einsum('rkgc,rckd->rkgd', weights.astype(jnp.bfloat16), values_old, p...]
  transfers between devices with their start and end apart: 3 -> 3, of which waited for: 2 -> 2; matrix products, arithmetic and copies ran while one was open for 12% -> 14% of each run, Pallas kernels for 9% -> 10%
where the time goes in v1:
time: 134 us; the launch traced here: 133 us
  blocking collectives  43.9 us (33%)
  Pallas kernels  22.7 us (17%)
  matrix products  18.2 us (14%)
  between operations  13.5 us (10%)
  other arithmetic  11.9 us (9%)
  starting transfers between devices  9.81 us (7%)
  waiting for transfers between devices  6.99 us (5%)
  local copies, waits for them, and re-layouts  6.37 us (5%)
    all_to_all x1, blocking collectives, on_device(): lax.all_to_all(delta_in, 'replica', split_axis=0, concat_axis=0, tiled=True)  28.6 us
    psum x1, blocking collectives, on_device(): shrunk_in = lax.psum(rank_part, ('tensor', 'sub')).astype(jnp.bfloat16)  15.3 us
    dot_general x1, matrix products, on_device(): jnp.dot(attended, output_projection, preferred_element_type=jnp.float32)  13.7 us
    another operation x2, Pallas kernels  12.4 us
    pallas_call x1, Pallas kernels, attend_local(): pl.pallas_call(attend_kernel, grid_spec=pltpu.PrefetchScalarGridSpec(num_...  9 us
    all_to_all x1, starting transfers between devices, on_device(): lax.all_to_all(labels, 'replica', split_axis=0, concat_axis=0, tiled=True)  6.32 us
    all_to_all x1, waiting for transfers between devices, on_device(): lax.all_to_all(outgoing, 'replica', split_axis=0, concat_axis=0, tiled=True)  4 us
    all_to_all x1, starting transfers between devices, on_device(): lax.all_to_all(outgoing, 'replica', split_axis=0, concat_axis=0, tiled=True)  3.49 us
  transfers between devices with their start and end apart: 3, of which 2 were waited for; matrix products, arithmetic and copies ran while one was open for 14% of the time, Pallas kernels for 10%

profile of v1, /device:TPU:0, one launch (start us, length us, event | category | flops | bytes accessed | tf_op | source)
XLA Modules:
  0.0 133.4 jit_solution(8927401993331911516)
XLA Ops:
  6.5 0.0 reduce-scatter.2.cloned.1.call-start
  6.5 9.0 %attend.1 = bf16[256,1024]{1,0:T(8,128)(2,1)} custom-call(s32[1]{0:T(128)} %bitcast.column_ref, s32[256]{0:T(256)} %length_ref.1, bf16[256,1024]{1,0:T(8,128)(2,1)} %query_ref.1, bf16[256,256]{1,0:T(8,128)(2,1)} %key_now_ref.1, bf16[256,256]{1,0:T(8,128)(2,1)} %value_now_ref.1, bf16[256,32,256]{2,1,0:T(8,128)(2,1)} %key_ref.1, bf16[256,32,256]{2,1,0:T(8,128)(2,1)} %value_ref.1), custom_call_target="tpu_custom_call" | custom-call | tf_op jit(solution)/shard_map/attend/pallas_call | solution.py:92
  15.5 13.7 %fusion.10 = f32[256,8192]{1,0:T(8,128)} fusion(bf16[256,1024]{1,0:T(8,128)(2,1)} %attend.1, bf16[1024,8192]{1,0:T(8,128)(2,1)} %param.19), kind=kOutput, calls=%fused_computation.44 | convolution fusion | flops 4294967296 | bytes 25690112 | tf_op jit(solution)/shard_map/dot_general | solution.py:140
  29.2 0.0 copy-start.2
  29.2 0.0 copy-start.3
  29.2 0.0 copy-start
  29.2 0.0 copy-start.1
  29.2 0.0 reduce-scatter.2.cloned.1.call-update
  29.3 0.6 copy-done.2
  29.9 0.0 copy-done.3
  29.9 0.1 select_reduce_fusion
  30.0 1.2 reduce-window.6
  31.3 0.1 slice.12
  31.3 0.1 copy.22
  31.5 0.1 copy.23
  31.6 0.1 add_bitcast_fusion
  31.7 0.2 fusion.3
  31.9 0.7 all_to_all.16
  32.6 6.3 %all-to-all-start = ((bf16[4,1,64]{2,1,0:T(2,128)(2,1)}), bf16[4,1,64]{2,1,0:T(2,128)(2,1)S(1)}, u32[]{:S(2)}, u32[]{:S(2)}) async-start(bf16[4,1,64]{2,1,0:T(2,128)(2,1)} %all_to_all.16), calls=%async_computation.1 | async-start | bytes 4096 | tf_op jit(solution)/shard_map/all_to_all | solution.py:173
  38.9 0.0 copy-done
  38.9 1.2 convolution_convert_fusion.1
  40.2 0.0 copy-done.1
  40.2 1.3 copy.25
  41.5 3.0 %all-to-all-done = bf16[4,1,64]{2,1,0:T(2,128)(2,1)S(1)} async-done(((bf16[4,1,64]{2,1,0:T(2,128)(2,1)}), bf16[4,1,64]{2,1,0:T(2,128)(2,1)S(1)}, u32[]{:S(2)}, u32[]{:S(2)}) %all-to-all-start) | async-done | bytes 544 | tf_op jit(solution)/shard_map/all_to_all | solution.py:173
  44.5 3.5 %all-to-all-start.1 = ((bf16[4,64,1024]{2,1,0:T(8,128)(2,1)}), bf16[4,64,1024]{2,1,0:T(8,128)(2,1)S(1)}, u32[]{:S(2)}, u32[]{:S(2)}) async-start(bf16[4,64,1024]{2,1,0:T(8,128)(2,1)} %bitcast.5), calls=%async_computation.2 | async-start | bytes 1048576 | tf_op jit(solution)/shard_map/all_to_all | solution.py:172
  48.0 0.1 reshape.85
  48.1 0.7 convert_reduce_fusion.1
  48.8 1.3 %ragged-dot-metadata = (s32[5]{0:T(128)}, s32[4]{0:T(128)}, s32[4]{0:T(128)}, s32[1]{0:T(128)}) custom-call(s32[4]{0:T(128)} %get-tuple-element.18), custom_call_target="tpu_custom_call" | custom-call | tf_op ragged-dot-metadata
  50.2 3.1 %sort.31 = (s32[256]{0:T(256)}, s32[256]{0:T(256)S(1)}) sort(s32[256]{0:T(256)S(1)} %compare_select_fusion.2, s32[256]{0:T(256)S(1)} %iota.46), dimensions={0}, to_apply=%region_6.7 | sort | flops 2048 | bytes 4096 | tf_op jit(solution)/shard_map/jit(argsort)/sort | solution.py:178
  53.3 3.1 %sort.32 = (s32[256]{0:T(256)}, s32[256]{0:T(256)S(1)}) sort(s32[256]{0:T(256)S(1)} %get-tuple-element.7, s32[256]{0:T(256)S(1)} %iota.47), dimensions={0}, to_apply=%region_9.10 | sort | flops 2048 | bytes 4096 | tf_op jit(solution)/shard_map/jit(argsort)/sort | solution.py:179
  56.4 0.6 iota_compare_fusion.6
  57.1 4.0 %all-to-all-done.1 = bf16[4,64,1024]{2,1,0:T(8,128)(2,1)S(1)} async-done(((bf16[4,64,1024]{2,1,0:T(8,128)(2,1)}), bf16[4,64,1024]{2,1,0:T(8,128)(2,1)S(1)}, u32[]{:S(2)}, u32[]{:S(2)}) %all-to-all-start.1) | async-done | bytes 524320 | tf_op jit(solution)/shard_map/all_to_all | solution.py:172
  61.1 2.0 %gather_fusion = bf16[256,1024]{1,0:T(8,128)(2,1)} fusion(bf16[256,1024]{1,0:T(8,128)(2,1)S(1)} %bitcast.38, s32[1024]{0:T(1024)S(1)} %pad_clamp_fusion.1), kind=kCustom, calls=%fused_computation | custom fusion | bytes 1049600 | tf_op jit(solution)/shard_map/gather | solution.py:180
  63.1 5.8 %ragged-dot-none.1 = f32[256,64]{1,0:T(8,128)} custom-call(s32[1]{0:T(128)} %get-tuple-element.9, s32[5]{0:T(128)} %get-tuple-element.10, s32[4]{0:T(128)} %get-tuple-element.11, s32[4]{0:T(128)} %get-tuple-element.12, s32[1]{0:T(128)} %get-tuple-element.9, bf16[256,1024]{1,0:T(8,128)(2,1)} %gather_fusion, bf16[4,1024,64]{2,1,0:T(8,128)(2,1)} %copy.25), custom_call_target="tpu_custom_call" | custom-call | flops 33554432 | bytes 1114128 | tf_op jit(solution)/shard_map/ragged_dot_general/ragged-dot-none
  68.9 1.0 broadcast_select_fusion
  69.9 15.3 %psum.7 = bf16[256,64]{1,0:T(8,128)(2,1)} all-reduce(f32[256,64]{1,0:T(8,128)S(1)} %broadcast_select_fusion), channel_id=1, replica_groups=mesh['group'=2,'replica'=4,'tensor'=2,'sub'=2] {'tensor','sub'}, use_global_device_ids=true, to_apply=%region_8.9 | all-reduce | flops 16384 | bytes 98304 | tf_op jit(solution)/shard_map/psum | solution.py:184
  85.2 6.6 %ragged-dot-none = f32[256,2048]{1,0:T(8,128)} custom-call(s32[1]{0:T(128)} %get-tuple-element.9, s32[5]{0:T(128)} %get-tuple-element.10, s32[4]{0:T(128)} %get-tuple-element.11, s32[4]{0:T(128)} %get-tuple-element.12, s32[1]{0:T(128)} %get-tuple-element.9, bf16[256,64]{1,0:T(8,128)(2,1)} %psum.7, bf16[4,64,2048]{2,1,0:T(8,128)(2,1)} %param.21), custom_call_target="tpu_custom_call" | custom-call | flops 67108864 | bytes 3178512 | tf_op jit(solution)/shard_map/ragged_dot_general/ragged-dot-none
  91.8 1.8 %select_convert_fusion = bf16[256,2048]{1,0:T(8,128)(2,1)S(1)} fusion(f32[256,2048]{1,0:T(8,128)} %ragged-dot-none, pred[256]{0:T(512)(128)(4,1)S(1)} %iota_compare_fusion.6), kind=kLoop, calls=%fused_computation.6 | loop fusion | flops 524288 | bytes 3145984 | tf_op jit(solution)/shard_map/convert_element_type | solution.py:185
  93.6 1.4 %gather_fusion.1 = bf16[256,2048]{1,0:T(8,128)(2,1)S(1)} fusion(bf16[256,2048]{1,0:T(8,128)(2,1)S(1)} %select_convert_fusion, s32[1024]{0:T(1024)S(1)} %pad_clamp_fusion), kind=kCustom, calls=%fused_computation.1 | custom fusion | bytes 2098176 | tf_op jit(solution)/shard_map/gather | solution.py:186
  94.9 28.6 %all_to_all.20 = bf16[4,64,2048]{2,1,0:T(8,128)(2,1)S(1)} all-to-all(bf16[4,64,2048]{2,1,0:T(8,128)(2,1)S(1)} %bitcast.40), channel_id=1, replica_groups=mesh['group'=2,'replica'=4,'tensor'=2,'sub'=2] {'replica'}, dimensions={0} | all-to-all | bytes 2097152 | tf_op jit(solution)/shard_map/all_to_all | solution.py:187
  123.5 0.0 reduce-scatter.2.cloned.1.call-done
  123.5 3.0 %fusion.2 = bf16[256,2048]{1,0:T(8,128)(2,1)} fusion(f32[256,2048]{1,0:T(8,128)} %reduce-scatter.2.cloned.1.call-done, bf16[256,2048]{1,0:T(8,128)(2,1)S(1)} %bitcast.39, s32[256]{0:T(256)S(1)} %multiply_add_fusion), kind=kOutput, calls=%fused_computation.5 | convolution fusion | flops 270598144 | bytes 4195328 | tf_op jit(solution)/shard_map/rs,sc->rc/dot_general | solution.py:188
  (18 shorter events, 0.2 us)
Async XLA Ops:
  6.5 117.0 %reduce-scatter.2.cloned.1.call-start = ((), (), s32[]{:S(2)}) async-start(), calls=%async_computation.4 | async-start | bytes 10485760 | tf_op jit(solution)/shard_map/reduce_scatter | solution.py:141
  29.2 0.7 copy-start.2
  29.2 0.7 copy-start.3
  29.2 9.7 %copy-start = (bf16[256,1024]{1,0:T(8,128)(2,1)S(1)}, bf16[256,1024]{1,0:T(8,128)(2,1)}, u32[]{:S(2)}) copy-start(bf16[256,1024]{1,0:T(8,128)(2,1)} %attend.1) | copy-start | bytes 1572868
  29.2 11.0 %copy-start.1 = (bf16[4,1024,64]{1,2,0:T(8,128)(2,1)S(1)}, bf16[4,1024,64]{1,2,0:T(8,128)(2,1)}, u32[]{:S(2)}) copy-start(bf16[4,1024,64]{1,2,0:T(8,128)(2,1)} %param.20) | copy-start | bytes 1572868
  32.6 11.9 %all-to-all-start = ((bf16[4,1,64]{2,1,0:T(2,128)(2,1)}), bf16[4,1,64]{2,1,0:T(2,128)(2,1)S(1)}, u32[]{:S(2)}, u32[]{:S(2)}) async-start(bf16[4,1,64]{2,1,0:T(2,128)(2,1)} %all_to_all.16), calls=%async_computation.1 | async-start | bytes 4096 | tf_op jit(solution)/shard_map/all_to_all | solution.py:173
  44.5 16.6 %all-to-all-start.1 = ((bf16[4,64,1024]{2,1,0:T(8,128)(2,1)}), bf16[4,64,1024]{2,1,0:T(8,128)(2,1)S(1)}, u32[]{:S(2)}, u32[]{:S(2)}) async-start(bf16[4,64,1024]{2,1,0:T(8,128)(2,1)} %bitcast.5), calls=%async_computation.2 | async-start | bytes 1048576 | tf_op jit(solution)/shard_map/all_to_all | solution.py:172
Sparse Core Ops, SparseCore 0:
  29.4 76.5 reduce-scatter.1

commit v2 on v1

--- a/solution.py
+++ b/solution.py
@@ -1,3 +1,5 @@
+import functools
+
 import jax
 import jax.numpy as jnp
 from jax import lax
@@ -10,6 +12,7 @@
 HEAD_WIDTH = 128
 CAP = 64
 LANES = 128
+MESH = pl.DeviceIdType.MESH
 
 
 def attend_kernel(
@@ -110,13 +113,291 @@
     )
 
 
-def grouped_product(rows_by_adapter, weights, group_sizes, leading_extent):
-    total_rows = rows_by_adapter.shape[0]
-    shifted = jnp.roll(rows_by_adapter, -leading_extent, axis=0)
-    result = lax.ragged_dot(shifted, weights, group_sizes, preferred_element_type=jnp.float32)
-    used = lax.broadcasted_iota(jnp.int32, (total_rows, 1), 0) < jnp.sum(group_sizes)
-    result = jnp.where(used, result, 0.0)
-    return jnp.roll(result, leading_extent, axis=0)
+def project_kernel(
+    tensors,
+    owners,
+    table_ref,
+    adapter_ref,
+    attended_ref,
+    projection_ref,
+    down_ref,
+    up_ref,
+    out_ref,
+    panel,
+    pair_out,
+    pair_in,
+    cross_out,
+    cross_in,
+    base,
+    route_out,
+    route_in,
+    rank_out,
+    rank_in,
+    delta_out,
+    delta_in,
+    gather,
+    panel_sem,
+    pair_send,
+    pair_recv,
+    cross_send,
+    cross_recv,
+    route_send,
+    route_recv,
+    rank_send,
+    rank_recv,
+    delta_send,
+    delta_recv,
+):
+    bf16, f32 = jnp.bfloat16, jnp.float32
+    replica = lax.axis_index("replica")
+    tensor = lax.axis_index("tensor")
+    sub = lax.axis_index("sub")
+    rows, feats = attended_ref.shape
+    chunk = panel.shape[2]
+    columns = out_ref.shape[1]
+    chunks = columns // chunk
+    peers = tensors * 2
+    far = (tensors - 1) * chunks
+    adp_local, _, rank = down_ref.shape
+    place = tensor * 2 + sub
+
+    def tensor_peer(e):
+        other = lax.rem(place + e, peers)
+        return {"tensor": other // 2, "sub": lax.rem(other, 2)}
+
+    barrier = pltpu.get_barrier_semaphore()
+    for e in range(1, peers):
+        pl.semaphore_signal(barrier, inc=1, device_id=tensor_peer(e), device_id_type=MESH)
+    for d in range(1, owners):
+        pl.semaphore_signal(
+            barrier, inc=1, device_id={"replica": lax.rem(replica + d, owners)}, device_id_type=MESH
+        )
+
+    def panel_copy(slot, other_tensor, other_sub, c):
+        start = pl.multiple_of((other_tensor * 2 + other_sub) * columns + c * chunk, chunk)
+        return pltpu.make_async_copy(
+            projection_ref.at[:, pl.ds(start, chunk)], panel.at[slot], panel_sem.at[slot]
+        )
+
+    def far_panel(i, mine):
+        other = lax.rem(tensor + 1 + i // chunks, tensors)
+        side = sub if mine else 1 - sub
+        return panel_copy(i + (far if mine else 0), other, side, lax.rem(i, chunks))
+
+    def near_panel(c, mine):
+        side = sub if mine else 1 - sub
+        return panel_copy(2 * far + (chunks if mine else 0) + c, tensor, side, c)
+
+    for i in range(far):
+        far_panel(i, False).start()
+    for i in range(far):
+        far_panel(i, True).start()
+    for c in range(chunks):
+        near_panel(c, False).start()
+    for c in range(chunks):
+        near_panel(c, True).start()
+
+    slots = owners * CAP
+    adapters = adapter_ref[...]
+    stored = jnp.zeros_like(adapters)
+    for a in range(table_ref.shape[0]):
+        stored = jnp.where(adapters == a, table_ref[a], stored)
+    owner = stored // adp_local
+    local = stored - owner * adp_local
+    step = lax.rem(owner - replica + owners, owners)
+    by_owner = lax.broadcasted_iota(jnp.int32, (max(owners, 8), rows), 0) == step
+    before = lax.broadcasted_iota(jnp.int32, (rows, rows), 0) < lax.broadcasted_iota(
+        jnp.int32, (rows, rows), 1
+    )
+    by_owner = jnp.where(by_owner, 1.0, 0.0)
+    earlier = jnp.dot(
+        by_owner.astype(bf16), jnp.where(before, 1.0, 0.0).astype(bf16), preferred_element_type=f32
+    )
+    position = jnp.sum(by_owner * earlier, axis=0, keepdims=True)
+    target = step.astype(f32) * CAP + position
+    slot_at = lax.broadcasted_iota(jnp.int32, (slots, rows), 0).astype(f32)
+    route = jnp.where(slot_at == target, 1.0, 0.0)
+    gather[...] = jnp.transpose(route).astype(bf16)
+    route = route.astype(bf16)
+    label = lax.broadcasted_iota(jnp.int32, (LANES, rows), 0) == local
+    label = jnp.where(label, 1.0, 0.0).astype(bf16)
+    labels = lax.dot_general(
+        route, label, (((1,), (1,)), ((), ())), preferred_element_type=f32
+    ).astype(bf16)
+    routed = jnp.dot(route, attended_ref[...], preferred_element_type=f32).astype(bf16)
+    for d in range(owners):
+        into = route_out.at[d] if d else route_in.at[0]
+        into[:, :feats] = routed[d * CAP : (d + 1) * CAP]
+        into[:, feats:] = labels[d * CAP : (d + 1) * CAP]
+
+    pl.semaphore_wait(barrier, peers - 1 + owners - 1)
+
+    def route_copy(d):
+        return pltpu.make_async_remote_copy(
+            src_ref=route_out.at[d],
+            dst_ref=route_in.at[d],
+            send_sem=route_send.at[d],
+            recv_sem=route_recv.at[d],
+            device_id={"replica": lax.rem(replica + d, owners)},
+            device_id_type=MESH,
+        )
+
+    def delta_copy(d):
+        return pltpu.make_async_remote_copy(
+            src_ref=delta_out.at[d],
+            dst_ref=delta_in.at[d],
+            send_sem=delta_send.at[d],
+            recv_sem=delta_recv.at[d],
+            device_id={"replica": lax.rem(replica - d + owners, owners)},
+            device_id_type=MESH,
+        )
+
+    def rank_copy(e):
+        return pltpu.make_async_remote_copy(
+            src_ref=rank_out,
+            dst_ref=rank_in.at[e],
+            send_sem=rank_send.at[e],
+            recv_sem=rank_recv.at[e],
+            device_id=tensor_peer(e),
+            device_id_type=MESH,
+        )
+
+    def pair_copy(i):
+        return pltpu.make_async_remote_copy(
+            src_ref=pair_out.at[i],
+            dst_ref=pair_in.at[i],
+            send_sem=pair_send.at[i],
+            recv_sem=pair_recv.at[i],
+            device_id={"sub": 1 - sub},
+            device_id_type=MESH,
+        )
+
+    def cross_copy(i):
+        return pltpu.make_async_remote_copy(
+            src_ref=cross_out.at[i],
+            dst_ref=cross_in.at[i],
+            send_sem=cross_send.at[i],
+            recv_sem=cross_recv.at[i],
+            device_id={"tensor": lax.rem(tensor + 1 + i // chunks, tensors)},
+            device_id_type=MESH,
+        )
+
+    for d in reversed(range(1, owners)):
+        route_copy(d).start()
+
+    def product(slot):
+        return jnp.dot(attended_ref[...], panel[slot], preferred_element_type=f32)
+
+    def far_pair(i, carry):
+        far_panel(i, False).wait()
+        pair_out[i] = product(i).astype(bf16)
+        pair_copy(i).start()
+        return carry
+
+    def far_mine(i, carry):
+        far_panel(i, True).wait()
+        mine = product(far + i)
+        pair_copy(i).wait_recv()
+        cross_out[i] = (mine + pair_in[i].astype(f32)).astype(bf16)
+        return carry
+
+    def far_send(i, carry):
+        cross_copy(i).start()
+        return carry
+
+    def far_both(i, carry):
+        return far_send(i, far_mine(i, carry))
+
+    def near_pair(c, carry):
+        near_panel(c, False).wait()
+        pair_out[far + c] = product(2 * far + c).astype(bf16)
+        pair_copy(far + c).start()
+        return carry
+
+    def near_mine(c, carry):
+        near_panel(c, True).wait()
+        base[c] = product(2 * far + chunks + c)
+        return carry
+
+    half = far // 2
+    lax.fori_loop(0, far, far_pair, 0)
+    lax.fori_loop(0, half, far_both, 0)
+    lax.fori_loop(half, far, far_mine, 0)
+    lax.fori_loop(0, chunks, near_pair, 0)
+    lax.fori_loop(0, chunks, near_mine, 0)
+
+    for d in reversed(range(1, owners)):
+        route_copy(d).wait_recv()
+    arrived = route_in[:, :, :feats].reshape(slots, feats)
+    marks = route_in[:, :, feats:].reshape(slots, LANES)
+    shrunk = jnp.zeros((slots, rank), f32)
+    for a in range(adp_local):
+        part = jnp.dot(arrived, down_ref[a], preferred_element_type=f32)
+        shrunk = shrunk + jnp.where(marks[:, a : a + 1].astype(f32) > 0.5, part, 0.0)
+    rank_out[...] = shrunk.astype(bf16)
+    for e in range(1, peers):
+        rank_copy(e).start()
+    wide = adp_local * rank
+    spread = lax.broadcasted_iota(jnp.int32, (LANES, wide), 0) == (
+        lax.broadcasted_iota(jnp.int32, (LANES, wide), 1) // rank
+    )
+    mask = jnp.dot(marks, jnp.where(spread, 1.0, 0.0).astype(bf16), preferred_element_type=f32)
+    repeat = lax.broadcasted_iota(jnp.int32, (rank, wide), 0) == lax.rem(
+        lax.broadcasted_iota(jnp.int32, (rank, wide), 1), rank
+    )
+    repeat = jnp.where(repeat, 1.0, 0.0).astype(bf16)
+    for e in range(1, peers):
+        rank_copy(e).wait_recv()
+        shrunk = shrunk + rank_in[e].astype(f32)
+    lax.fori_loop(half, far, far_send, 0)
+    held = jnp.dot(shrunk.astype(bf16), repeat, preferred_element_type=f32)
+    held = jnp.where(mask > 0.5, held, 0.0).astype(bf16)
+    for d in reversed(range(owners)):
+        into = delta_out if d else delta_in
+        into[d] = jnp.dot(
+            held[d * CAP : (d + 1) * CAP], up_ref[...], preferred_element_type=f32
+        ).astype(bf16)
+        if d:
+            delta_copy(d).start()
+
+    def near_add(c, carry):
+        pair_copy(far + c).wait_recv()
+        base[c] = base[c] + pair_in[far + c].astype(f32)
+        return carry
+
+    def far_add(i, carry):
+        cross_copy(i).wait_recv()
+        c = lax.rem(i, chunks)
+        base[c] = base[c] + cross_in[i].astype(f32)
+        return carry
+
+    lax.fori_loop(0, chunks, near_add, 0)
+    lax.fori_loop(0, far, far_add, 0)
+    for d in range(1, owners):
+        delta_copy(d).wait_recv()
+    for c in range(chunks):
+        at = slice(c * chunk, (c + 1) * chunk)
+        delta = jnp.dot(
+            gather[...], delta_in[:, :, at].reshape(slots, chunk), preferred_element_type=f32
+        )
+        out_ref[:, at] = (base[c] + delta).astype(bf16)
+
+    for d in range(1, owners):
+        route_copy(d).wait_send()
+        delta_copy(d).wait_send()
+    for e in range(1, peers):
+        rank_copy(e).wait_send()
+
+    def pair_sent(i, carry):
+        pair_copy(i).wait_send()
+        return carry
+
+    def cross_sent(i, carry):
+        cross_copy(i).wait_send()
+        return carry
+
+    lax.fori_loop(0, far + chunks, pair_sent, 0)
+    lax.fori_loop(0, far, cross_sent, 0)
 
 
 def on_device(
@@ -132,67 +413,71 @@
     adapter_down_weights,
     adapter_up_weights,
 ):
-    row_count = queries.shape[0]
-    feat_count = queries.shape[1]
     attended = attend_local(
         queries, incoming_keys, incoming_values, cached_key_rows, cached_value_rows, cache_length
     )
-    partial_out = jnp.dot(attended, output_projection, preferred_element_type=jnp.float32)
-    base = lax.psum_scatter(partial_out, ("tensor", "sub"), scatter_dimension=1, tiled=True)
-    output_columns = adapter_up_weights.shape[2]
-    adp_local = adapter_down_weights.shape[0]
-    adapter_count = adapter_slot_table.shape[0]
-    matched = adapter_of_row[:, None] == lax.broadcasted_iota(
-        jnp.int32, (row_count, adapter_count), 1
-    )
-    slot_of_row = jnp.sum(jnp.where(matched, adapter_slot_table[None, :], 0), axis=1)
+    rows, feats = attended.shape
+    adp_local, _, rank = adapter_down_weights.shape
+    columns = adapter_up_weights.shape[2]
+    tensors = lax.axis_size("tensor")
     owners = lax.axis_size("replica")
-    owner_of_row = slot_of_row // adp_local
-    local_id = slot_of_row - owner_of_row * adp_local
-    by_owner = (
-        owner_of_row[:, None] == lax.broadcasted_iota(jnp.int32, (row_count, owners), 1)
-    ).astype(jnp.int32)
-    earlier = jnp.cumsum(by_owner, axis=0) - by_owner
-    position = jnp.sum(earlier * by_owner, axis=1)
-    target = owner_of_row * CAP + position
-    slot_total = owners * CAP
-    route_map = (
-        target[:, None] == lax.broadcasted_iota(jnp.int32, (row_count, slot_total), 1)
-    ).astype(jnp.bfloat16)
-    outgoing = jnp.einsum("rs,rf->sf", route_map, attended, preferred_element_type=jnp.float32)
-    outgoing = outgoing.astype(jnp.bfloat16).reshape(owners, CAP, feat_count)
-    labels = jnp.einsum(
-        "rs,r->s",
-        route_map,
-        (local_id + 1).astype(jnp.bfloat16),
-        preferred_element_type=jnp.float32,
-    )
-    labels = labels.astype(jnp.bfloat16).reshape(owners, CAP)
-    arrived, arrived_labels = (
-        lax.all_to_all(outgoing, "replica", split_axis=0, concat_axis=0, tiled=True),
-        lax.all_to_all(labels, "replica", split_axis=0, concat_axis=0, tiled=True),
-    )
-    arrived_rows = arrived.reshape(slot_total, feat_count)
-    label_ids = arrived_labels.reshape(slot_total).astype(jnp.int32)
-    sort_keys = jnp.where(label_ids == 0, adp_local + 1, label_ids)
-    order_in = jnp.argsort(sort_keys, stable=True)
-    inverse_in = jnp.argsort(order_in, stable=True)
-    sorted_in = arrived_rows[order_in]
-    wanted = lax.broadcasted_iota(jnp.int32, (1, adp_local), 1) + 1
-    sizes_in = jnp.sum((label_ids[:, None] == wanted).astype(jnp.int32), axis=0)
-    rank_part = grouped_product(sorted_in, adapter_down_weights, sizes_in, 0)
-    shrunk_in = lax.psum(rank_part, ("tensor", "sub")).astype(jnp.bfloat16)
-    delta_sorted = grouped_product(shrunk_in, adapter_up_weights, sizes_in, 0).astype(jnp.bfloat16)
-    delta_in = delta_sorted[inverse_in].reshape(owners, CAP, output_columns)
-    returned = lax.all_to_all(delta_in, "replica", split_axis=0, concat_axis=0, tiled=True)
-    delta = jnp.einsum(
-        "rs,sc->rc",
-        route_map,
-        returned.reshape(slot_total, output_columns),
-        preferred_element_type=jnp.float32,
-    )
-    delta = delta.astype(jnp.bfloat16)
-    return (base + delta.astype(jnp.float32)).astype(jnp.bfloat16)
+    peers = tensors * lax.axis_size("sub")
+    chunk = min(512, columns)
+    chunks = columns // chunk
+    far = (tensors - 1) * chunks
+    bf16 = jnp.bfloat16
+    vmem = pl.BlockSpec(memory_space=pltpu.VMEM)
+    dma = pltpu.SemaphoreType.DMA
+    return pl.pallas_call(
+        functools.partial(project_kernel, tensors, owners),
+        out_shape=jax.ShapeDtypeStruct((rows, columns), bf16),
+        in_specs=[
+            pl.BlockSpec(memory_space=pltpu.SMEM),
+            vmem,
+            vmem,
+            pl.BlockSpec(memory_space=pl.ANY),
+            vmem,
+            vmem,
+        ],
+        out_specs=vmem,
+        scratch_shapes=[
+            pltpu.VMEM((peers * chunks, feats, chunk), bf16),
+            pltpu.VMEM((far + chunks, rows, chunk), bf16),
+            pltpu.VMEM((far + chunks, rows, chunk), bf16),
+            pltpu.VMEM((far, rows, chunk), bf16),
+            pltpu.VMEM((far, rows, chunk), bf16),
+            pltpu.VMEM((chunks, rows, chunk), jnp.float32),
+            pltpu.VMEM((owners, CAP, feats + LANES), bf16),
+            pltpu.VMEM((owners, CAP, feats + LANES), bf16),
+            pltpu.VMEM((owners * CAP, rank), bf16),
+            pltpu.VMEM((peers, owners * CAP, rank), bf16),
+            pltpu.VMEM((owners, CAP, columns), bf16),
+            pltpu.VMEM((owners, CAP, columns), bf16),
+            pltpu.VMEM((rows, owners * CAP), bf16),
+            dma((peers * chunks,)),
+            dma((far + chunks,)),
+            dma((far + chunks,)),
+            dma((far,)),
+            dma((far,)),
+            dma((owners,)),
+            dma((owners,)),
+            dma((peers,)),
+            dma((peers,)),
+            dma((owners,)),
+            dma((owners,)),
+        ],
+        compiler_params=pltpu.CompilerParams(
+            collective_id=0, has_side_effects=True, vmem_limit_bytes=52 * 1024 * 1024
+        ),
+        name="project",
+    )(
+        adapter_slot_table,
+        adapter_of_row.reshape(1, rows),
+        attended,
+        output_projection,
+        adapter_down_weights,
+        adapter_up_weights.reshape(adp_local * rank, columns),
+    )
 
 
 def solution(mesh):

time: 134 us -> 62 us (0.46)
  the two profiles are of different devices: /device:TPU:0 before, /device:TPU:9 now
where the time goes in v2:
time: 62 us; the launch traced here: 61.8 us
  Pallas kernels  58.4 us (94%)
  local copies, waits for them, and re-layouts  3.34 us (5%)
    pallas_call x1, Pallas kernels, on_device(): pl.pallas_call(functools.partial(project_kernel, tensors, owners), out_sh...  49.3 us
    pallas_call x1, Pallas kernels, attend_local(): pl.pallas_call(attend_kernel, grid_spec=pltpu.PrefetchScalarGridSpec(num_...  9.13 us
    unnamed x10, local copies, waits for them, and re-layouts  3.34 us

profile of v2, /device:TPU:9, one launch (start us, length us, event | category | flops | bytes accessed | tf_op | source)
XLA Modules:
  0.0 61.8 jit_solution(14778951667303564284)
XLA Ops:
  0.0 0.0 copy-start.3
  0.0 0.0 copy-start.1
  0.0 0.0 copy-start.2
  0.0 9.1 %attend.1.attended_ref = bf16[256,1024]{1,0:T(8,128)(2,1)} custom-call(s32[1]{0:T(128)} %bitcast.1.column_ref, s32[256]{0:T(256)} %length_ref.1, bf16[256,1024]{1,0:T(8,128)(2,1)} %query_ref.1, bf16[256,256]{1,0:T(8,128)(2,1)} %key_now_ref.1, bf16[256,256]{1,0:T(8,128)(2,1)} %value_now_ref.1, bf16[256,32,256]{2,1,0:T(8,128)(2,1)} %key_ref.1, ...), custom_call_target="tpu_custom_call" | custom-call | tf_op jit(solution)/shard_map/attend/pallas_call | solution.py:95
  9.1 0.0 copy-done.3
  9.1 1.3 %copy.12.down_ref = bf16[4,1024,64]{2,1,0:T(8,128)(2,1)} copy(bf16[4,1024,64]{1,2,0:T(8,128)(2,1)S(1)} %copy-done.3) | data formatting | bytes 1048576 | tf_op args[9]
  10.5 0.0 copy-done.1
  10.5 0.0 copy-done.2
  10.5 0.0 copy-start
  10.5 1.0 %copy-done = bf16[256,1024]{1,0:T(8,128)(2,1)S(1)} copy-done((bf16[256,1024]{1,0:T(8,128)(2,1)S(1)}, bf16[256,1024]{1,0:T(8,128)(2,1)}, u32[]{:S(2)}) %copy-start) | copy-done | bytes 524312
  11.5 49.3 %project.1 = bf16[256,2048]{1,0:T(8,128)(2,1)S(1)} custom-call(s32[16]{0:T(128)S(1)} %copy-done.2, s32[1,256]{1,0:T(1,128)S(1)} %bitcast.3, bf16[256,1024]{1,0:T(8,128)(2,1)S(1)} %copy-done, bf16[1024,8192]{1,0:T(8,128)(2,1)} %projection_ref.1, bf16[4,1024,64]{2,1,0:T(8,128)(2,1)} %copy.12.down_ref, bf16[256,2048]{1,0:T(8,128)(2,1)} %bitcast.4), custom_call_target="tpu_custom_call" | custom-call | tf_op jit(solution)/shard_map/project/pallas_call | solution.py:431
  60.8 1.0 %copy.14 = bf16[256,2048]{1,0:T(8,128)(2,1)} copy(bf16[256,2048]{1,0:T(8,128)(2,1)S(1)} %project.1) | data formatting | bytes 2097152
Async XLA Ops:
  0.0 9.1 %copy-start.3 = (bf16[4,1024,64]{1,2,0:T(8,128)(2,1)S(1)}, bf16[4,1024,64]{1,2,0:T(8,128)(2,1)}, u32[]{:S(2)}) copy-start(bf16[4,1024,64]{1,2,0:T(8,128)(2,1)} %param.20) | copy-start | bytes 1572868
  0.0 10.5 %copy-start.1 = (s32[256]{0:T(256)S(1)}, s32[256]{0:T(256)}, u32[]{:S(2)}) copy-start(s32[256]{0:T(256)} %param.17) | copy-start | bytes 3076
  0.0 10.5 %copy-start.2 = (s32[16]{0:T(128)S(1)}, s32[16]{0:T(128)}, u32[]{:S(2)}) copy-start(s32[16]{0:T(128)} %table_ref.1) | copy-start | bytes 196
  10.5 1.0 %copy-start = (bf16[256,1024]{1,0:T(8,128)(2,1)S(1)}, bf16[256,1024]{1,0:T(8,128)(2,1)}, u32[]{:S(2)}) copy-start(bf16[256,1024]{1,0:T(8,128)(2,1)} %attend.1.attended_ref) | copy-start | bytes 1572868

commit v3 on v2

--- a/solution.py
+++ b/solution.py
@@ -12,18 +12,17 @@
 HEAD_WIDTH = 128
 CAP = 64
 LANES = 128
+PARTS = 2
 MESH = pl.DeviceIdType.MESH
 
 
-def attend_kernel(
-    column_ref, length_ref, query_ref, key_now_ref, value_now_ref, key_ref, value_ref, out_ref
+def attend_block(
+    first_row, block, length_ref, query_ref, key_now_ref, value_now_ref, key_ref, value_ref, out_ref
 ):
-    block = query_ref.shape[0]
     heads = query_ref.shape[1] // HEAD_WIDTH
     context = key_ref.shape[1]
     rows = LANES // heads
     copies = LANES // context
-    first_row = pl.program_id(0) * block
     lane = lax.broadcasted_iota(jnp.int32, (1, LANES), 1)
     lane_row = lax.rem(lane, rows)
     row_masks = [lane_row == r for r in range(rows)]
@@ -35,7 +34,7 @@
     score_scale = HEAD_WIDTH ** (-0.5)
     contract_last = (((1,), (1,)), ((), ()))
     for group in range(block // rows):
-        at = slice(group * rows, (group + 1) * rows)
+        at = pl.ds(pl.multiple_of(first_row + group * rows, rows), rows)
         stacked = jnp.concatenate(
             [query_ref[at, h * HEAD_WIDTH : (h + 1) * HEAD_WIDTH] for h in range(heads)], axis=0
         )
@@ -80,49 +79,28 @@
             out_ref[at, h * HEAD_WIDTH : (h + 1) * HEAD_WIDTH] = attended[h * rows : (h + 1) * rows]
 
 
-def attend_local(
-    queries, incoming_keys, incoming_values, cached_key_rows, cached_value_rows, cache_length
-):
-    row_count, feat_count = queries.shape
-    context = cached_key_rows.shape[1]
-    heads = feat_count // HEAD_WIDTH
-    first_kv = lax.axis_index("sub") * heads // (QUERY_HEADS // KV_HEADS)
-    column = first_kv.astype(jnp.int32).reshape(1)
-    block = 64
-    now_spec = pl.BlockSpec((block, HEAD_WIDTH), lambda i, c, n: (i, c[0]))
-    old_spec = pl.BlockSpec((block, context, HEAD_WIDTH), lambda i, c, n: (i, 0, c[0]))
-    row_spec = pl.BlockSpec((block, feat_count), lambda i, c, n: (i, 0))
-    return pl.pallas_call(
-        attend_kernel,
-        grid_spec=pltpu.PrefetchScalarGridSpec(
-            num_scalar_prefetch=2,
-            grid=(row_count // block,),
-            in_specs=[row_spec, now_spec, now_spec, old_spec, old_spec],
-            out_specs=row_spec,
-        ),
-        out_shape=jax.ShapeDtypeStruct((row_count, feat_count), jnp.bfloat16),
-        name="attend",
-    )(
-        column,
-        cache_length,
-        queries,
-        incoming_keys,
-        incoming_values,
-        cached_key_rows,
-        cached_value_rows,
-    )
-
-
 def project_kernel(
     tensors,
     owners,
     table_ref,
+    length_ref,
     adapter_ref,
-    attended_ref,
+    query_ref,
+    fresh_key_ref,
+    fresh_value_ref,
+    stored_key_ref,
+    stored_value_ref,
     projection_ref,
+    stored_down_ref,
+    stored_up_ref,
+    out_ref,
+    key_now_ref,
+    value_now_ref,
+    key_ref,
+    value_ref,
     down_ref,
     up_ref,
-    out_ref,
+    attended_ref,
     panel,
     pair_out,
     pair_in,
@@ -131,11 +109,15 @@
     base,
     route_out,
     route_in,
+    label_out,
+    label_in,
     rank_out,
     rank_in,
     delta_out,
     delta_in,
     gather,
+    cache_sem,
+    weight_sem,
     panel_sem,
     pair_send,
     pair_recv,
@@ -143,6 +125,8 @@
     cross_recv,
     route_send,
     route_recv,
+    label_send,
+    label_recv,
     rank_send,
     rank_recv,
     delta_send,
@@ -153,12 +137,21 @@
     tensor = lax.axis_index("tensor")
     sub = lax.axis_index("sub")
     rows, feats = attended_ref.shape
+    block = min(64, rows)
+    heads = feats // HEAD_WIDTH
+    head_at = pl.ds(
+        pl.multiple_of(sub * heads // (QUERY_HEADS // KV_HEADS) * HEAD_WIDTH, HEAD_WIDTH), HEAD_WIDTH
+    )
     chunk = panel.shape[2]
     columns = out_ref.shape[1]
     chunks = columns // chunk
     peers = tensors * 2
     far = (tensors - 1) * chunks
-    adp_local, _, rank = down_ref.shape
+    rank = rank_out.shape[2]
+    wide = down_ref.shape[0]
+    adp_local = wide // rank
+    part_cap = CAP // PARTS
+    part_slots = owners * part_cap
     place = tensor * 2 + sub
 
     def tensor_peer(e):
@@ -188,6 +181,30 @@
         side = sub if mine else 1 - sub
         return panel_copy(2 * far + (chunks if mine else 0) + c, tensor, side, c)
 
+    def cache_copies(i):
+        at = pl.ds(pl.multiple_of(i * block, block), block)
+        return [
+            pltpu.make_async_copy(
+                stored.at[at, :, head_at], kept.at[at], cache_sem.at[2 * i + which]
+            )
+            for which, (stored, kept) in enumerate(
+                [(stored_key_ref, key_ref), (stored_value_ref, value_ref)]
+            )
+        ]
+
+    weight_copies = [
+        pltpu.make_async_copy(stored_down_ref, down_ref, weight_sem.at[0]),
+        pltpu.make_async_copy(stored_up_ref, up_ref, weight_sem.at[1]),
+    ]
+    now_copies = [
+        pltpu.make_async_copy(fresh_key_ref.at[:, head_at], key_now_ref, weight_sem.at[2]),
+        pltpu.make_async_copy(fresh_value_ref.at[:, head_at], value_now_ref, weight_sem.at[3]),
+    ]
+    for copy in now_copies:
+        copy.start()
+    for i in range(rows // block):
+        for copy in cache_copies(i):
+            copy.start()
     for i in range(far):
         far_panel(i, False).start()
     for i in range(far):
@@ -196,6 +213,8 @@
         near_panel(c, False).start()
     for c in range(chunks):
         near_panel(c, True).start()
+    for copy in weight_copies:
+        copy.start()
 
     slots = owners * CAP
     adapters = adapter_ref[...]
@@ -214,7 +233,11 @@
         by_owner.astype(bf16), jnp.where(before, 1.0, 0.0).astype(bf16), preferred_element_type=f32
     )
     position = jnp.sum(by_owner * earlier, axis=0, keepdims=True)
-    target = step.astype(f32) * CAP + position
+    target = step.astype(f32) * part_cap + position
+    for part in range(1, PARTS):
+        target = target + jnp.where(position >= part * part_cap, 1.0, 0.0) * (
+            part_slots - part_cap
+        )
     slot_at = lax.broadcasted_iota(jnp.int32, (slots, rows), 0).astype(f32)
     route = jnp.where(slot_at == target, 1.0, 0.0)
     gather[...] = jnp.transpose(route).astype(bf16)
@@ -224,40 +247,50 @@
     labels = lax.dot_general(
         route, label, (((1,), (1,)), ((), ())), preferred_element_type=f32
     ).astype(bf16)
-    routed = jnp.dot(route, attended_ref[...], preferred_element_type=f32).astype(bf16)
-    for d in range(owners):
-        into = route_out.at[d] if d else route_in.at[0]
-        into[:, :feats] = routed[d * CAP : (d + 1) * CAP]
-        into[:, feats:] = labels[d * CAP : (d + 1) * CAP]
+    for part in range(PARTS):
+        for d in range(owners):
+            into = label_out if d else label_in
+            first = part * part_slots + d * part_cap
+            into[d, part] = labels[first : first + part_cap]
 
     pl.semaphore_wait(barrier, peers - 1 + owners - 1)
 
-    def route_copy(d):
+    def label_copy(d):
         return pltpu.make_async_remote_copy(
-            src_ref=route_out.at[d],
-            dst_ref=route_in.at[d],
-            send_sem=route_send.at[d],
-            recv_sem=route_recv.at[d],
+            src_ref=label_out.at[d],
+            dst_ref=label_in.at[d],
+            send_sem=label_send.at[d],
+            recv_sem=label_recv.at[d],
             device_id={"replica": lax.rem(replica + d, owners)},
             device_id_type=MESH,
         )
 
-    def delta_copy(d):
+    def route_copy(part, d):
         return pltpu.make_async_remote_copy(
-            src_ref=delta_out.at[d],
-            dst_ref=delta_in.at[d],
-            send_sem=delta_send.at[d],
-            recv_sem=delta_recv.at[d],
+            src_ref=route_out.at[part, d],
+            dst_ref=route_in.at[part, d],
+            send_sem=route_send.at[part, d],
+            recv_sem=route_recv.at[part, d],
+            device_id={"replica": lax.rem(replica + d, owners)},
+            device_id_type=MESH,
+        )
+
+    def delta_copy(part, d):
+        return pltpu.make_async_remote_copy(
+            src_ref=delta_out.at[part, d],
+            dst_ref=delta_in.at[part, d],
+            send_sem=delta_send.at[part, d],
+            recv_sem=delta_recv.at[part, d],
             device_id={"replica": lax.rem(replica - d + owners, owners)},
             device_id_type=MESH,
         )
 
-    def rank_copy(e):
+    def rank_copy(part, e):
         return pltpu.make_async_remote_copy(
-            src_ref=rank_out,
-            dst_ref=rank_in.at[e],
-            send_sem=rank_send.at[e],
-            recv_sem=rank_recv.at[e],
+            src_ref=rank_out.at[part],
+            dst_ref=rank_in.at[part, e],
+            send_sem=rank_send.at[part, e],
+            recv_sem=rank_recv.at[part, e],
             device_id=tensor_peer(e),
             device_id_type=MESH,
         )
@@ -282,8 +315,40 @@
             device_id_type=MESH,
         )
 
-    for d in reversed(range(1, owners)):
-        route_copy(d).start()
+    for d in range(1, owners):
+        label_copy(d).start()
+
+    for copy in now_copies:
+        copy.wait()
+
+    def attend_rows(i, carry):
+        for copy in cache_copies(i):
+            copy.wait()
+        attend_block(
+            i * block,
+            block,
+            length_ref,
+            query_ref,
+            key_now_ref,
+            value_now_ref,
+            key_ref,
+            value_ref,
+            attended_ref,
+        )
+        return carry
+
+    lax.fori_loop(0, rows // block, attend_rows, 0)
+    for part in range(PARTS):
+        routed = jnp.dot(
+            route[part * part_slots : (part + 1) * part_slots],
+            attended_ref[...],
+            preferred_element_type=f32,
+        ).astype(bf16)
+        for d in reversed(range(owners)):
+            into = route_out if d else route_in
+            into[part, d] = routed[d * part_cap : (d + 1) * part_cap]
+            if d:
+                route_copy(part, d).start()
 
     def product(slot):
         return jnp.dot(attended_ref[...], panel[slot], preferred_element_type=f32)
@@ -319,46 +384,62 @@
         base[c] = product(2 * far + chunks + c)
         return carry
 
-    half = far // 2
-    lax.fori_loop(0, far, far_pair, 0)
-    lax.fori_loop(0, half, far_both, 0)
-    lax.fori_loop(half, far, far_mine, 0)
-    lax.fori_loop(0, chunks, near_pair, 0)
-    lax.fori_loop(0, chunks, near_mine, 0)
-
-    for d in reversed(range(1, owners)):
-        route_copy(d).wait_recv()
-    arrived = route_in[:, :, :feats].reshape(slots, feats)
-    marks = route_in[:, :, feats:].reshape(slots, LANES)
-    shrunk = jnp.zeros((slots, rank), f32)
-    for a in range(adp_local):
-        part = jnp.dot(arrived, down_ref[a], preferred_element_type=f32)
-        shrunk = shrunk + jnp.where(marks[:, a : a + 1].astype(f32) > 0.5, part, 0.0)
-    rank_out[...] = shrunk.astype(bf16)
-    for e in range(1, peers):
-        rank_copy(e).start()
-    wide = adp_local * rank
     spread = lax.broadcasted_iota(jnp.int32, (LANES, wide), 0) == (
         lax.broadcasted_iota(jnp.int32, (LANES, wide), 1) // rank
     )
-    mask = jnp.dot(marks, jnp.where(spread, 1.0, 0.0).astype(bf16), preferred_element_type=f32)
+    spread = jnp.where(spread, 1.0, 0.0).astype(bf16)
     repeat = lax.broadcasted_iota(jnp.int32, (rank, wide), 0) == lax.rem(
         lax.broadcasted_iota(jnp.int32, (rank, wide), 1), rank
     )
     repeat = jnp.where(repeat, 1.0, 0.0).astype(bf16)
-    for e in range(1, peers):
-        rank_copy(e).wait_recv()
-        shrunk = shrunk + rank_in[e].astype(f32)
-    lax.fori_loop(half, far, far_send, 0)
-    held = jnp.dot(shrunk.astype(bf16), repeat, preferred_element_type=f32)
-    held = jnp.where(mask > 0.5, held, 0.0).astype(bf16)
-    for d in reversed(range(owners)):
-        into = delta_out if d else delta_in
-        into[d] = jnp.dot(
-            held[d * CAP : (d + 1) * CAP], up_ref[...], preferred_element_type=f32
-        ).astype(bf16)
-        if d:
-            delta_copy(d).start()
+
+    def shrink(part):
+        for d in reversed(range(1, owners)):
+            route_copy(part, d).wait_recv()
+        arrived = route_in[part].reshape(part_slots, feats)
+        marks = label_in[:, part].reshape(part_slots, LANES)
+        mask = jnp.dot(marks, spread, preferred_element_type=f32)
+        product = lax.dot_general(
+            arrived, down_ref[...], (((1,), (1,)), ((), ())), preferred_element_type=f32
+        )
+        product = jnp.where(mask > 0.5, product, 0.0)
+        shrunk = product[:, :rank]
+        for a in range(1, adp_local):
+            shrunk = shrunk + product[:, a * rank : (a + 1) * rank]
+        rank_out[part] = shrunk.astype(bf16)
+        for e in range(1, peers):
+            rank_copy(part, e).start()
+        return shrunk, mask
+
+    def expand(part, shrunk, mask):
+        for e in range(1, peers):
+            rank_copy(part, e).wait_recv()
+            shrunk = shrunk + rank_in[part, e].astype(f32)
+        held = jnp.dot(shrunk.astype(bf16), repeat, preferred_element_type=f32)
+        held = jnp.where(mask > 0.5, held, 0.0).astype(bf16)
+        delta = jnp.dot(held, up_ref[...], preferred_element_type=f32).astype(bf16)
+        for d in reversed(range(owners)):
+            into = delta_out if d else delta_in
+            into[part, d] = delta[d * part_cap : (d + 1) * part_cap]
+            if d:
+                delta_copy(part, d).start()
+
+    first, second = far // 4, far // 2
+    lax.fori_loop(0, far, far_pair, 0)
+    lax.fori_loop(0, first, far_both, 0)
+    lax.fori_loop(first, far, far_mine, 0)
+    for copy in weight_copies:
+        copy.wait()
+    for d in range(1, owners):
+        label_copy(d).wait_recv()
+    early = shrink(0)
+    lax.fori_loop(0, chunks, near_pair, 0)
+    expand(0, *early)
+    lax.fori_loop(first, second, far_send, 0)
+    late = shrink(1)
+    lax.fori_loop(0, chunks, near_mine, 0)
+    expand(1, *late)
+    lax.fori_loop(second, far, far_send, 0)
 
     def near_add(c, carry):
         pair_copy(far + c).wait_recv()
@@ -373,20 +454,29 @@
 
     lax.fori_loop(0, chunks, near_add, 0)
     lax.fori_loop(0, far, far_add, 0)
+    for part in range(PARTS):
+        for d in range(1, owners):
+            delta_copy(part, d).wait_recv()
+        for c in range(chunks):
+            at = slice(c * chunk, (c + 1) * chunk)
+            total = base[c] + jnp.dot(
+                gather[:, part * part_slots : (part + 1) * part_slots],
+                delta_in[part, :, :, at].reshape(part_slots, chunk),
+                preferred_element_type=f32,
+            )
+            if part < PARTS - 1:
+                base[c] = total
+            else:
+                out_ref[:, at] = total.astype(bf16)
+
     for d in range(1, owners):
-        delta_copy(d).wait_recv()
-    for c in range(chunks):
-        at = slice(c * chunk, (c + 1) * chunk)
-        delta = jnp.dot(
-            gather[...], delta_in[:, :, at].reshape(slots, chunk), preferred_element_type=f32
-        )
-        out_ref[:, at] = (base[c] + delta).astype(bf16)
-
-    for d in range(1, owners):
-        route_copy(d).wait_send()
-        delta_copy(d).wait_send()
+        label_copy(d).wait_send()
+        for part in range(PARTS):
+            route_copy(part, d).wait_send()
+            delta_copy(part, d).wait_send()
     for e in range(1, peers):
-        rank_copy(e).wait_send()
+        for part in range(PARTS):
+            rank_copy(part, e).wait_send()
 
     def pair_sent(i, carry):
         pair_copy(i).wait_send()
@@ -413,10 +503,8 @@
     adapter_down_weights,
     adapter_up_weights,
 ):
-    attended = attend_local(
-        queries, incoming_keys, incoming_values, cached_key_rows, cached_value_rows, cache_length
-    )
-    rows, feats = attended.shape
+    rows, feats = queries.shape
+    context = cached_key_rows.shape[1]
     adp_local, _, rank = adapter_down_weights.shape
     columns = adapter_up_weights.shape[2]
     tensors = lax.axis_size("tensor")
@@ -427,44 +515,53 @@
     far = (tensors - 1) * chunks
     bf16 = jnp.bfloat16
     vmem = pl.BlockSpec(memory_space=pltpu.VMEM)
+    smem = pl.BlockSpec(memory_space=pltpu.SMEM)
+    hbm = pl.BlockSpec(memory_space=pl.ANY)
+    part_cap = CAP // PARTS
     dma = pltpu.SemaphoreType.DMA
     return pl.pallas_call(
         functools.partial(project_kernel, tensors, owners),
         out_shape=jax.ShapeDtypeStruct((rows, columns), bf16),
-        in_specs=[
-            pl.BlockSpec(memory_space=pltpu.SMEM),
-            vmem,
-            vmem,
-            pl.BlockSpec(memory_space=pl.ANY),
-            vmem,
-            vmem,
-        ],
+        in_specs=[smem, smem, vmem, vmem, hbm, hbm, hbm, hbm, hbm, hbm, hbm],
         out_specs=vmem,
         scratch_shapes=[
+            pltpu.VMEM((rows, HEAD_WIDTH), bf16),
+            pltpu.VMEM((rows, HEAD_WIDTH), bf16),
+            pltpu.VMEM((rows, context, HEAD_WIDTH), bf16),
+            pltpu.VMEM((rows, context, HEAD_WIDTH), bf16),
+            pltpu.VMEM((adp_local * rank, feats), bf16),
+            pltpu.VMEM((adp_local * rank, columns), bf16),
+            pltpu.VMEM((rows, feats), bf16),
             pltpu.VMEM((peers * chunks, feats, chunk), bf16),
             pltpu.VMEM((far + chunks, rows, chunk), bf16),
             pltpu.VMEM((far + chunks, rows, chunk), bf16),
             pltpu.VMEM((far, rows, chunk), bf16),
             pltpu.VMEM((far, rows, chunk), bf16),
             pltpu.VMEM((chunks, rows, chunk), jnp.float32),
-            pltpu.VMEM((owners, CAP, feats + LANES), bf16),
-            pltpu.VMEM((owners, CAP, feats + LANES), bf16),
-            pltpu.VMEM((owners * CAP, rank), bf16),
-            pltpu.VMEM((peers, owners * CAP, rank), bf16),
-            pltpu.VMEM((owners, CAP, columns), bf16),
-            pltpu.VMEM((owners, CAP, columns), bf16),
+            pltpu.VMEM((PARTS, owners, part_cap, feats), bf16),
+            pltpu.VMEM((PARTS, owners, part_cap, feats), bf16),
+            pltpu.VMEM((owners, PARTS, part_cap, LANES), bf16),
+            pltpu.VMEM((owners, PARTS, part_cap, LANES), bf16),
+            pltpu.VMEM((PARTS, owners * part_cap, rank), bf16),
+            pltpu.VMEM((PARTS, peers, owners * part_cap, rank), bf16),
+            pltpu.VMEM((PARTS, owners, part_cap, columns), bf16),
+            pltpu.VMEM((PARTS, owners, part_cap, columns), bf16),
             pltpu.VMEM((rows, owners * CAP), bf16),
+            dma((2 * rows // min(64, rows),)),
+            dma((4,)),
             dma((peers * chunks,)),
             dma((far + chunks,)),
             dma((far + chunks,)),
             dma((far,)),
             dma((far,)),
+            dma((PARTS, owners)),
+            dma((PARTS, owners)),
             dma((owners,)),
             dma((owners,)),
-            dma((peers,)),
-            dma((peers,)),
-            dma((owners,)),
-            dma((owners,)),
+            dma((PARTS, peers)),
+            dma((PARTS, peers)),
+            dma((PARTS, owners)),
+            dma((PARTS, owners)),
         ],
         compiler_params=pltpu.CompilerParams(
             collective_id=0, has_side_effects=True, vmem_limit_bytes=52 * 1024 * 1024
@@ -472,10 +569,15 @@
         name="project",
     )(
         adapter_slot_table,
+        cache_length,
         adapter_of_row.reshape(1, rows),
-        attended,
+        queries,
+        incoming_keys,
+        incoming_values,
+        cached_key_rows,
+        cached_value_rows,
         output_projection,
-        adapter_down_weights,
+        jnp.swapaxes(adapter_down_weights, 1, 2).reshape(adp_local * rank, feats),
         adapter_up_weights.reshape(adp_local * rank, columns),
     )
 

time: 62 us -> 61.7 us (level)
  the two profiles are of different devices: /device:TPU:9 before, /device:TPU:0 now
where the time goes in v3:
time: 61.7 us; the launch traced here: 61.3 us
  Pallas kernels  53.1 us (86%)
  local copies, waits for them, and re-layouts  8.21 us (13%)
    pallas_call x1, Pallas kernels, on_device(): pl.pallas_call(functools.partial(project_kernel, tensors, owners), out_sh...  53.1 us
    unnamed x15, local copies, waits for them, and re-layouts  8.21 us

profile of v3, /device:TPU:0, one launch (start us, length us, event | category | flops | bytes accessed | tf_op | source)
XLA Modules:
  0.0 61.3 jit_solution(17472720724703159753)
XLA Ops:
  0.0 0.0 copy-start
  0.0 1.0 %copy-done = bf16[256,1024]{1,0:T(8,128)(2,1)S(1)} copy-done((bf16[256,1024]{1,0:T(8,128)(2,1)S(1)}, bf16[256,1024]{1,0:T(8,128)(2,1)}, u32[]{:S(2)}) %copy-start) | copy-done | bytes 524312
  1.0 0.0 copy-start.1
  1.0 1.0 %copy-done.1 = bf16[4,1024,64]{1,2,0:T(8,128)(2,1)S(1)} copy-done((bf16[4,1024,64]{1,2,0:T(8,128)(2,1)S(1)}, bf16[4,1024,64]{1,2,0:T(8,128)(2,1)}, u32[]{:S(2)}) %copy-start.1) | copy-done | bytes 524312
  2.1 0.0 copy-start.2
  2.1 0.9 %copy-done.2 = bf16[256,256]{1,0:T(8,128)(2,1)S(1)} copy-done((bf16[256,256]{1,0:T(8,128)(2,1)S(1)}, bf16[256,256]{1,0:T(8,128)(2,1)}, u32[]{:S(2)}) %copy-start.2) | copy-done | bytes 131096
  3.0 0.0 copy-start.3
  3.0 0.9 %copy-done.3 = bf16[256,256]{1,0:T(8,128)(2,1)S(1)} copy-done((bf16[256,256]{1,0:T(8,128)(2,1)S(1)}, bf16[256,256]{1,0:T(8,128)(2,1)}, u32[]{:S(2)}) %copy-start.3) | copy-done | bytes 131096
  3.9 0.0 copy-start.4
  3.9 0.7 %copy-done.4 = s32[256]{0:T(256)S(1)} copy-done((s32[256]{0:T(256)S(1)}, s32[256]{0:T(256)}, u32[]{:S(2)}) %copy-start.4) | copy-done | bytes 1048
  4.6 0.0 copy-start.5
  4.6 0.7 %copy-done.5 = s32[256]{0:T(256)S(1)} copy-done((s32[256]{0:T(256)S(1)}, s32[256]{0:T(256)}, u32[]{:S(2)}) %copy-start.5) | copy-done | bytes 1048
  5.3 0.0 copy-start.6
  5.3 0.7 %copy-done.6 = s32[16]{0:T(128)S(1)} copy-done((s32[16]{0:T(128)S(1)}, s32[16]{0:T(128)}, u32[]{:S(2)}) %copy-start.6) | copy-done | bytes 88
  5.9 53.1 %project.1 = bf16[256,2048]{1,0:T(8,128)(2,1)} custom-call(s32[16]{0:T(128)S(1)} %copy-done.6, s32[256]{0:T(256)S(1)} %copy-done.4, s32[1,256]{1,0:T(1,128)S(1)} %bitcast.6, bf16[256,1024]{1,0:T(8,128)(2,1)S(1)} %copy-done, bf16[256,256]{1,0:T(8,128)(2,1)S(1)} %copy-done.2, bf16[256,256]{1,0:T(8,128)(2,1)S(1)} %copy-done.3, ...), custom_call_target="tpu_custom_call" | custom-call | tf_op jit(solution)/shard_map/project/pallas_call | solution.py:522
  59.0 2.3 %copy.13 = bf16[256,2048]{1,0:T(8,128)(2,1)} copy(bf16[256,2048]{1,0:T(8,128)(2,1)} %project.1) | data formatting | bytes 2097152
Async XLA Ops:
  0.0 1.0 %copy-start = (bf16[256,1024]{1,0:T(8,128)(2,1)S(1)}, bf16[256,1024]{1,0:T(8,128)(2,1)}, u32[]{:S(2)}) copy-start(bf16[256,1024]{1,0:T(8,128)(2,1)} %query_ref.1) | copy-start | bytes 1572868
  1.0 1.0 %copy-start.1 = (bf16[4,1024,64]{1,2,0:T(8,128)(2,1)S(1)}, bf16[4,1024,64]{1,2,0:T(8,128)(2,1)}, u32[]{:S(2)}) copy-start(bf16[4,1024,64]{1,2,0:T(8,128)(2,1)} %param.20) | copy-start | bytes 1572868
  2.1 0.9 %copy-start.2 = (bf16[256,256]{1,0:T(8,128)(2,1)S(1)}, bf16[256,256]{1,0:T(8,128)(2,1)}, u32[]{:S(2)}) copy-start(bf16[256,256]{1,0:T(8,128)(2,1)} %fresh_key_ref.1) | copy-start | bytes 393220
  3.0 0.9 %copy-start.3 = (bf16[256,256]{1,0:T(8,128)(2,1)S(1)}, bf16[256,256]{1,0:T(8,128)(2,1)}, u32[]{:S(2)}) copy-start(bf16[256,256]{1,0:T(8,128)(2,1)} %fresh_value_ref.1) | copy-start | bytes 393220
  3.9 0.7 %copy-start.4 = (s32[256]{0:T(256)S(1)}, s32[256]{0:T(256)}, u32[]{:S(2)}) copy-start(s32[256]{0:T(256)} %length_ref.1) | copy-start | bytes 3076
  4.6 0.7 %copy-start.5 = (s32[256]{0:T(256)S(1)}, s32[256]{0:T(256)}, u32[]{:S(2)}) copy-start(s32[256]{0:T(256)} %param.17) | copy-start | bytes 3076
  5.3 0.7 %copy-start.6 = (s32[16]{0:T(128)S(1)}, s32[16]{0:T(128)}, u32[]{:S(2)}) copy-start(s32[16]{0:T(128)} %table_ref.1) | copy-start | bytes 196

commit v4 on v3

--- a/solution.py
+++ b/solution.py
@@ -424,22 +424,21 @@
             if d:
                 delta_copy(part, d).start()
 
-    first, second = far // 4, far // 2
+    first = far // 4
     lax.fori_loop(0, far, far_pair, 0)
     lax.fori_loop(0, first, far_both, 0)
-    lax.fori_loop(first, far, far_mine, 0)
     for copy in weight_copies:
         copy.wait()
     for d in range(1, owners):
         label_copy(d).wait_recv()
     early = shrink(0)
+    lax.fori_loop(first, far, far_mine, 0)
+    late = shrink(1)
+    lax.fori_loop(first, far, far_send, 0)
+    expand(0, *early)
+    expand(1, *late)
     lax.fori_loop(0, chunks, near_pair, 0)
-    expand(0, *early)
-    lax.fori_loop(first, second, far_send, 0)
-    late = shrink(1)
     lax.fori_loop(0, chunks, near_mine, 0)
-    expand(1, *late)
-    lax.fori_loop(second, far, far_send, 0)
 
     def near_add(c, carry):
         pair_copy(far + c).wait_recv()
@@ -564,7 +563,7 @@
             dma((PARTS, owners)),
         ],
         compiler_params=pltpu.CompilerParams(
-            collective_id=0, has_side_effects=True, vmem_limit_bytes=52 * 1024 * 1024
+            collective_id=0, has_side_effects=True, vmem_limit_bytes=63 * 1024 * 1024
         ),
         name="project",
     )(

time: 61.7 us -> 57 us (0.924)
  local copies, waits for them, and re-layouts: 8.21 us -> 2.3 us
  Pallas kernels: 53.1 us -> 53.9 us
    unnamed x15 -> x1, local copies, waits for them, and re-layouts: 8.21 us -> 2.3 us
    pallas_call x1, Pallas kernels: 53.1 us -> 53.9 us  [on_device(): pl.pallas_call(functools.partial(project_kernel, tensors, owners), out_sh...]
where the time goes in v4:
time: 57 us; the launch traced here: 56.2 us
  Pallas kernels  53.9 us (95%)
  local copies, waits for them, and re-layouts  2.3 us (4%)
    pallas_call x1, Pallas kernels, on_device(): pl.pallas_call(functools.partial(project_kernel, tensors, owners), out_sh...  53.9 us
    unnamed x1, local copies, waits for them, and re-layouts  2.3 us

profile of v4, /device:TPU:0, one launch (start us, length us, event | category | flops | bytes accessed | tf_op | source)
XLA Modules:
  0.0 56.2 jit_solution(3312181485943972980)
XLA Ops:
  0.0 53.9 %project.1 = bf16[256,2048]{1,0:T(8,128)(2,1)} custom-call(s32[16]{0:T(128)} %table_ref.1, s32[256]{0:T(256)} %length_ref.1, s32[1,256]{1,0:T(1,128)} %bitcast.7, bf16[256,1024]{1,0:T(8,128)(2,1)} %query_ref.1, bf16[256,256]{1,0:T(8,128)(2,1)} %fresh_key_ref.1, bf16[256,256]{1,0:T(8,128)(2,1)} %fresh_value_ref.1, bf16[256,32,256]{2,1,0:T(8,128)(2,1)} %stored_key_ref.1, ...), custom_call_target="tpu_custom_call" | custom-call | tf_op jit(solution)/shard_map/project/pallas_call | solution.py:521
  53.9 2.3 %copy.13 = bf16[256,2048]{1,0:T(8,128)(2,1)} copy(bf16[256,2048]{1,0:T(8,128)(2,1)} %project.1) | data formatting | bytes 2097152
